TPU v7x, 32 devices: a whole 2x2x4 slice. The times are simulated.
32 devices in a mesh: groups: 2 (over x), tm: 16 (over z, y, core).
Axes of the slice: x: 2, y: 2, z: 4, core: 2. Of those that a mesh axis runs over, the one named last changes fastest.
Arguments:
- sharded_latents: bfloat16 [32, 6144], P('groups', 'tm'), parts along dimension 0, may hold values from -6 to 6
- sample_frame_count: int32 [16], P('groups'), parts along dimension 0, may hold values from 5 to 8, as said below
- entry_kernel: bfloat16 [27, 16, 384], replicated, may hold values from -0.3125 to 0.3125
- entry_bias: float32 [384], replicated, may hold values from -3 to 3
- norm_scale_gain: float32 [384], replicated, may hold values from 0.25 to 1.75
- residual_kernel: bfloat16 [27, 384, 384], P(None, 'tm'), may hold values from -0.0625 to 0.0625
- residual_bias: float32 [384], replicated, may hold values from -3 to 3
Outputs:
- decoded: bfloat16 [128, 6, 16, 384], P(('groups', 'tm')), parts along dimension 0
There are 2 independent parts, one for each index of `groups`. A program takes and returns all parts, laid end to end along the dimension named above; an argument that names none is the same for every part. Nothing has to cross between parts.
Inputs may be any that keep to these rules, and one draw needn't show every extreme that they name: `sample_frame_count`: every sample has more than half of its 8 frames valid; some sample has all of them valid.
All inputs are finite; a program needn't handle non-finite values.
Results may differ from a plain program's by a relative error of at most 0.009.
Values may be sent and summed in bfloat16 or wider, within the bound.
A program may use at most 64 MiB of HBM per device.

v0:
```python
import jax
import jax.numpy as jnp
from jax import lax
from jax.experimental import pallas as pl
from jax.experimental.pallas import tpu as pltpu
from jax.sharding import PartitionSpec as P

LATENT_CHANNELS = 16
C = 384
PROMPT_SAMPLES = 8
BLOCK_FRAMES = 4
LATENT_ROWS = 6
LATENT_COLUMNS = 16


def from_behind(block, axis, distance):
    devices = range(lax.axis_size(axis))
    route = [(i - distance, i) for i in devices if i - distance in devices]
    return lax.ppermute(block, axis, route)


def causal_conv(frames, weight):
    frames_out = frames.shape[0] - 2
    inputs = frames.shape[3]
    padded = jnp.pad(frames, ((0, 0), (1, 1), (1, 1), (0, 0)))
    total = jnp.zeros((frames_out * LATENT_ROWS * LATENT_COLUMNS, weight.shape[2]), jnp.float32)
    for time_tap in range(3):
        for row_tap in range(3):
            for col_tap in range(3):
                window = padded[
                    time_tap : time_tap + frames_out,
                    row_tap : row_tap + LATENT_ROWS,
                    col_tap : col_tap + LATENT_COLUMNS,
                    :,
                ]
                window = window.reshape(frames_out * LATENT_ROWS * LATENT_COLUMNS, inputs)
                tap = 9 * time_tap + 3 * row_tap + col_tap
                total = total + jnp.dot(window, weight[tap], preferred_element_type=jnp.float32)
    return total


def activate(stream, norm_scale_gain):
    values = stream.astype(jnp.float32)
    scale = lax.rsqrt(jnp.mean(values * values, axis=-1, keepdims=True) + 1e-06)
    return jax.nn.silu(values * scale * norm_scale_gain).astype(jnp.bfloat16)


def to_cells(planes):
    return jnp.transpose(
        planes.reshape(planes.shape[0], LATENT_CHANNELS, LATENT_ROWS, LATENT_COLUMNS), (0, 2, 3, 1)
    )


def shards(
    sharded_latents,
    sample_frame_count,
    entry_kernel,
    entry_bias,
    norm_scale_gain,
    residual_kernel,
    residual_bias,
):
    gathered_latents = lax.all_to_all(
        sharded_latents, "tm", split_axis=0, concat_axis=1, tiled=True
    )
    latent_volume = gathered_latents.reshape(
        BLOCK_FRAMES, LATENT_CHANNELS, LATENT_ROWS * LATENT_COLUMNS
    )
    position = lax.axis_index("tm")
    block = position // PROMPT_SAMPLES
    sample = position % PROMPT_SAMPLES
    keep = block > 0
    earlier = from_behind(latent_volume, "tm", PROMPT_SAMPLES)
    earlier = jnp.where(keep, earlier, jnp.zeros_like(earlier))
    frames = to_cells(jnp.concatenate([earlier, latent_volume], axis=0))
    widened = (causal_conv(frames, entry_kernel) + entry_bias).astype(jnp.bfloat16)
    active_all = activate(widened, norm_scale_gain).reshape(
        BLOCK_FRAMES + 2, LATENT_ROWS, LATENT_COLUMNS, C
    )
    behind = jnp.where(keep, active_all[:2], jnp.zeros_like(active_all[:2]))
    extended = jnp.concatenate([behind, active_all[2:]], axis=0)
    stream = widened[2 * LATENT_ROWS * LATENT_COLUMNS :]
    kernel_all = lax.all_gather(residual_kernel, "tm", axis=1, tiled=True)
    branch = causal_conv(extended, kernel_all)
    total = (stream.astype(jnp.float32) + (branch + residual_bias)).reshape(
        BLOCK_FRAMES, LATENT_ROWS, LATENT_COLUMNS, C
    )
    limit = jnp.sum(jnp.where(jnp.arange(PROMPT_SAMPLES) == sample, sample_frame_count, 0))
    frame_index = block * BLOCK_FRAMES + jnp.arange(BLOCK_FRAMES)
    valid = (frame_index < limit)[:, None, None, None]
    return jnp.where(valid, total, jnp.zeros_like(total)).astype(jnp.bfloat16)


MESH = pl.DeviceIdType.MESH
F32, BF16 = jnp.float32, jnp.bfloat16
CELLS = LATENT_ROWS * LATENT_COLUMNS
PLANE = 128
SLICES = 3
TAPS = 7


def section_kernel(
    latq, counts, entry_far, entry_bias_far, gain_far, residual_bias_far, pieces,
    out,
    entry, entry_bias, gain, residual_bias, lat, at, act, kept, weights, acc, done,
    lat_send, lat_recv, z_send, z_recv, p_send, p_recv, c_send, c_recv, o_send, o_recv, own,
):
    x = lax.axis_index("groups")
    me = lax.axis_index("tm")
    z, y, c = me // 4, (me // 2) % 2, me % 2
    quarter = 2 * x + c
    across = 2 * (1 - x) + c

    def where_(zz, yy, cc):
        return {"tm": zz * 4 + yy * 2 + cc}

    peers = [
        {"groups": x, "tm": z * 4 + (1 - y) * 2 + c},
        {"groups": 1 - x, "tm": me},
        {"groups": 1 - x, "tm": z * 4 + (1 - y) * 2 + c},
    ]
    sibling = {"tm": z * 4 + y * 2 + (1 - c)}

    barrier = pltpu.get_barrier_semaphore()
    for step in range(1, 16):
        pl.semaphore_signal(barrier, inc=1, device_id={"tm": lax.rem(me + step, 16)}, device_id_type=MESH)
    for peer in peers[1:]:
        pl.semaphore_signal(barrier, inc=1, device_id=peer, device_id_type=MESH)
    pl.semaphore_wait(barrier, 17)

    def remote(src, dst, send, recv, device):
        return pltpu.make_async_remote_copy(
            src_ref=src, dst_ref=dst, send_sem=send, recv_sem=recv, device_id=device, device_id_type=MESH
        )

    def lat_copy(to):
        return remote(latq.at[to % 4], lat.at[me], lat_send.at[to], lat_recv.at[me], {"tm": to})

    def rows_of(zz, yy):
        return pl.ds(pl.multiple_of(48 * (2 * zz + yy), 16), 48)

    def z_copy(n):
        return remote(
            pieces.at[n], weights.at[quarter, :, rows_of(z, y), :], z_send.at[n], z_recv.at[z], where_(n, y, c)
        )

    def z_arrival(zz):
        return remote(
            pieces.at[0], weights.at[quarter, :, rows_of(zz, y), :], z_send.at[0], z_recv.at[zz], where_(zz, y, c)
        )

    def p_copy(r, zz, source=None):
        block = weights.at[quarter, :, rows_of(zz, y), :]
        return remote(block if source is None else source, block, p_send.at[r, zz], p_recv.at[r, zz], peers[r])

    def p_arrival(r, zz):
        block = weights.at[quarter if r == 0 else across, :, rows_of(zz, y if r == 1 else 1 - y), :]
        return remote(block, block, p_send.at[r, zz], p_recv.at[r, zz], peers[r])

    def c_block(core, r, zz):
        which = 2 * (x if r < 2 else 1 - x) + core
        return weights.at[which, :, rows_of(zz, y if r % 2 == 0 else 1 - y), :]

    def c_copy(r, zz, source=None):
        block = c_block(c, r, zz)
        return remote(block if source is None else source, block, c_send.at[r, zz], c_recv.at[r, zz], sibling)

    def c_arrival(r, zz):
        block = c_block(1 - c, r, zz)
        return remote(block, block, c_send.at[r, zz], c_recv.at[r, zz], sibling)

    def columns(n):
        return pl.ds(pl.multiple_of(128 * n, 128), 128)

    def o_copy(d):
        return remote(done.at[d], out.at[:, columns(z)], o_send.at[d], o_recv.at[z], where_(d, y, c))

    def o_arrival(n):
        return remote(done.at[0], out.at[:, columns(n)], o_send.at[0], o_recv.at[n], where_(n, y, c))

    for to in range(12):
        @pl.when(to != me)
        def _():
            lat_copy(to).start()

    for n in range(SLICES):
        @pl.when(n != z)
        def _():
            z_copy(n).start()

    @pl.when(z < SLICES)
    def _():
        own_piece = pieces.at[lax.rem(z, SLICES)]
        for r in range(3):
            p_copy(r, z, own_piece).start()
        c_copy(0, z, own_piece).start()
        mine = [
            pltpu.make_async_copy(latq.at[me % 4], lat.at[me], own.at[0]),
            pltpu.make_async_copy(own_piece, weights.at[quarter, :, rows_of(z, y), :], own.at[1]),
            pltpu.make_async_copy(entry_far, entry, own.at[2]),
            pltpu.make_async_copy(entry_bias_far, entry_bias, own.at[3]),
            pltpu.make_async_copy(gain_far, gain, own.at[4]),
            pltpu.make_async_copy(residual_bias_far, residual_bias, own.at[5]),
        ]
        for copy in mine:
            copy.start()

        def forward(step):
            near = jnp.where(z == 2, 3 - step, step + jnp.where(step >= z, 1, 0))
            near = jnp.where((z == 2) & (step == 0), 3, near)
            near = jnp.where((z == 2) & (step > 0), 2 - step, near)
            z_arrival(near).wait_recv()
            for r in range(3):
                p_copy(r, near).start()
            c_copy(0, near).start()

        at[:, 0:2] = jnp.zeros((2, 2, 144, PLANE), BF16)
        act[:, :, 0:2] = jnp.zeros((3, 2, 2, PLANE, C), BF16)
        act[:, :, 2:, 0:16] = jnp.zeros((3, 2, 8, 16, C), BF16)
        act[:, :, 2:, 112:128] = jnp.zeros((3, 2, 8, 16, C), BF16)
        forward(0)
        for copy in mine:
            copy.wait()
        for source in range(16):
            @pl.when(source != me)
            def _():
                remote(latq.at[0], lat.at[source], lat_send.at[0], lat_recv.at[source], {"tm": source}).wait_recv()
        target = lax.broadcasted_iota(jnp.int32, (256, 256), 0)
        origin = lax.broadcasted_iota(jnp.int32, (256, 256), 1)
        h_, b_, g_, ch_ = target // 128, (target // 64) % 2, (target // 16) % 4, target % 16
        perm = (origin == (g_ * 4 + ch_ // 4) * 16 + (b_ * 2 + h_) * 4 + ch_ % 4).astype(F32).astype(BF16)
        cells = jnp.dot(perm, lat[...].reshape(256, PLANE), preferred_element_type=F32)
        lane = lax.broadcasted_iota(jnp.int32, (256, PLANE), 1)
        row, column = lane // LATENT_COLUMNS, lane % LATENT_COLUMNS
        for j in range(3):
            for k in range(3):
                offset = (j - 1) * LATENT_COLUMNS + (k - 1)
                moved = pltpu.roll(cells, (-offset) % PLANE, 1) if offset else cells
                good = (
                    (row + (j - 1) >= 0)
                    & (row + (j - 1) < LATENT_ROWS)
                    & (column + (k - 1) >= 0)
                    & (column + (k - 1) < LATENT_COLUMNS)
                )
                tap = 3 * j + k
                at[:, 2:, tap * 16 : tap * 16 + 16, :] = (
                    jnp.where(good, moved, 0.0).astype(BF16).reshape(2, 8, 16, PLANE)
                )

        def inlet(index, carry):
            h, f = index // 8, index % 8
            left = at[h, pl.ds(f, 3)].reshape(432, PLANE)
            wide = lax.dot_general(left, entry[...], (((0,), (0,)), ((), ())), preferred_element_type=F32)
            stream = (wide[:CELLS] + entry_bias[...][None, :]).astype(BF16)
            kept[index] = stream
            values = stream.astype(F32)
            scale = lax.rsqrt(jnp.mean(values * values, axis=-1, keepdims=True) + 1e-06)
            u = values * scale * gain[...][None, :]
            active = (u / (1.0 + jnp.exp(-u))).astype(BF16).astype(F32)
            column = lax.broadcasted_iota(jnp.int32, (CELLS, C), 0) % LATENT_COLUMNS
            act[1, h, 2 + f, 16:112] = active.astype(BF16)
            act[0, h, 2 + f, 16:112] = jnp.where(column == 0, 0.0, pltpu.roll(active, 1, 0)).astype(BF16)
            act[2, h, 2 + f, 16:112] = jnp.where(
                column == LATENT_COLUMNS - 1, 0.0, pltpu.roll(active, CELLS - 1, 0)
            ).astype(BF16)
            return carry

        lax.fori_loop(0, 4, inlet, 0)
        forward(1)
        lax.fori_loop(4, 10, inlet, 0)
        forward(2)
        lax.fori_loop(10, 16, inlet, 0)

        def taps_of(which, d, total):
            h, b = d % 2, d // 2
            for low, count in ((0, 7),):
                lefts = []
                for t in range(low, low + count):
                    tap = jnp.minimum(which * TAPS + t, 26)
                    i, j, k = tap // 9, (tap // 3) % 3, tap % 3
                    left = act[k, h, pl.ds(4 * b + i, 4), pl.ds(pl.multiple_of(16 * j, 16), CELLS), :]
                    lefts.append(left.reshape(4 * CELLS, C))
                right = weights[which, low : low + count].reshape(count * C, 128)
                total = total + jnp.dot(jnp.concatenate(lefts, axis=1), right, preferred_element_type=F32)
            return total

        def sweep(which, first):
            def body(d, carry):
                start = jnp.zeros((4 * CELLS, 128), F32) if first else acc[d]
                acc[d] = taps_of(which, d, start)
                return carry

            lax.fori_loop(0, 4, body, 0)

        for zz in range(4):
            p_arrival(0, zz).wait_recv()
            c_copy(1, zz).start()
        sweep(quarter, True)
        for zz in range(4):
            for r in (1, 2):
                p_arrival(r, zz).wait_recv()
                c_copy(1 + r, zz).start()
        for r in (0, 1):
            for zz in range(4):
                c_arrival(r, zz).wait_recv()
        sweep(2 * x + 1 - c, False)
        sweep(across, False)
        for r in (2, 3):
            for zz in range(4):
                c_arrival(r, zz).wait_recv()
        last = 2 * (1 - x) + 1 - c

        def finish(step, carry):
            middle = jnp.where(step == 0, 3, jnp.where(step == 1, 0, jnp.where(step == 2, 2, 1)))
            upper = jnp.where(step < 2, step, 5 - step)
            d = jnp.where(z == 0, 3 - step, jnp.where(z == 1, middle, upper))
            h, b = d % 2, d // 2
            total = taps_of(last, d, acc[d])
            stream = kept[pl.ds(h * 8 + b * 4, 4), :, columns(z)].astype(F32)
            total = stream + (total + residual_bias[columns(z)][None, :]).reshape(4, CELLS, 128)
            limit = counts[me % 4 + 4 * h]
            valid = lax.broadcasted_iota(jnp.int32, (4, CELLS, 128), 0) + 4 * b < limit
            done[d] = jnp.where(valid, total, 0.0).astype(BF16).reshape(4 * CELLS, 128)

            @pl.when(d != z)
            def _():
                o_copy(d).start()

            return carry

        lax.fori_loop(0, 4, finish, 0)
        out[:, columns(z)] = done[z]

    for n in range(SLICES):
        @pl.when(n != z)
        def _():
            o_arrival(n).wait_recv()
            z_copy(n).wait_send()

    for to in range(12):
        @pl.when(to != me)
        def _():
            lat_copy(to).wait_send()

    @pl.when(z < SLICES)
    def _():
        for r in range(3):
            for zz in range(4):
                p_copy(r, zz).wait_send()
        for r in range(4):
            for zz in range(4):
                c_copy(r, zz).wait_send()
        for d in range(4):
            @pl.when(d != z)
            def _():
                o_copy(d).wait_send()


def sliced_shards(
    sharded_latents,
    sample_frame_count,
    entry_kernel,
    entry_bias,
    norm_scale_gain,
    residual_kernel,
    residual_bias,
):
    x, me = lax.axis_index("groups"), lax.axis_index("tm")
    c = me % 2
    quarters = jnp.pad(residual_kernel, ((0, 1), (0, 0), (0, 0)))
    mine = lax.dynamic_slice_in_dim(quarters, (2 * x + c) * TAPS, TAPS, 0)
    theirs = lax.dynamic_slice_in_dim(quarters, (2 * x + 1 - c) * TAPS, TAPS, 0)
    received = lax.ppermute(theirs, "tm", [(i, i ^ 1) for i in range(16)])
    low = jnp.where(c == 0, mine, received)
    high = jnp.where(c == 0, received, mine)
    both = jnp.concatenate([low, high], axis=1)
    pieces = jnp.transpose(both.reshape(TAPS, 48, SLICES, 128), (2, 0, 1, 3))

    latq = jnp.transpose(sharded_latents.reshape(4, 4, 4, CELLS), (1, 0, 2, 3)).reshape(4, 16, CELLS)
    latq = jnp.pad(latq, ((0, 0), (0, 0), (0, PLANE - CELLS)))
    vmem = pl.BlockSpec(memory_space=pltpu.VMEM)
    far = pl.BlockSpec(memory_space=pltpu.HBM)
    dma = pltpu.SemaphoreType.DMA
    out = pl.pallas_call(
        section_kernel,
        out_shape=jax.ShapeDtypeStruct((4 * CELLS, C), BF16),
        in_specs=[vmem, pl.BlockSpec(memory_space=pltpu.SMEM)] + [far] * 4 + [vmem],
        out_specs=vmem,
        scratch_shapes=[
            pltpu.VMEM((27 * LATENT_CHANNELS, C), BF16),
            pltpu.VMEM((C,), F32), pltpu.VMEM((C,), F32), pltpu.VMEM((C,), F32),
            pltpu.VMEM((16, 16, PLANE), BF16),
            pltpu.VMEM((2, 10, 144, PLANE), BF16),
            pltpu.VMEM((3, 2, 10, PLANE, C), BF16),
            pltpu.VMEM((16, CELLS, C), BF16),
            pltpu.VMEM((4, TAPS, C, 128), BF16),
            pltpu.VMEM((4, 4 * CELLS, 128), F32),
            pltpu.VMEM((4, 4 * CELLS, 128), BF16),
            dma((12,)), dma((16,)), dma((3,)), dma((4,)), dma((3, 4)), dma((3, 4)),
            dma((4, 4)), dma((4, 4)), dma((4,)), dma((3,)), dma((6,)),
        ],
        compiler_params=pltpu.CompilerParams(
            collective_id=0, has_side_effects=True, vmem_limit_bytes=40 * 1024 * 1024
        ),
        cost_estimate=pl.CostEstimate(flops=5_000_000_000, bytes_accessed=2_000_000, transcendentals=600_000),
    )(
        latq,
        sample_frame_count,
        entry_kernel.reshape(27 * LATENT_CHANNELS, C),
        entry_bias,
        norm_scale_gain,
        residual_bias,
        pieces,
    )
    return out.reshape(4, LATENT_ROWS, LATENT_COLUMNS, C)


def solution(mesh):
    in_specs = (P("groups", "tm"), P("groups"), P(), P(), P(), P(None, "tm", None), P())
    out_specs = P(("groups", "tm"), None, None, None)
    sliced = mesh.shape["groups"] == 2 and mesh.shape["tm"] == 16
    body = sliced_shards if sliced else shards
    return jax.shard_map(body, mesh=mesh, in_specs=in_specs, out_specs=out_specs, check_vma=False)
```

profile of v0, /device:TPU:18, one launch (start us, length us, event | category | flops | bytes accessed | tf_op | source)
XLA Modules:
  0.0 46.5 jit_solution(1400959691221625861)
XLA Ops:
  0.0 0.0 copy-start.5
  0.0 0.0 copy-start.6
  0.0 1.0 %pad_dynamic-slice_fusion = bf16[7,24,384]{2,1,0:T(8,128)(2,1)S(1)} fusion(s32[]{:T(128)S(6)} %select_n.28, bf16[27,24,384]{2,1,0:T(8,128)(2,1)} %param.12), kind=kLoop, calls=%fused_computation | loop fusion | bytes 626692 | tf_op jit(solution)/shard_map/dynamic_slice | solution.py:372
  1.0 0.1 collective-permute-start
  1.1 0.0 copy-done.6
  1.1 0.1 reshape.15
  1.2 1.2 %collective-permute-done = bf16[7,24,384]{2,1,0:T(8,128)(2,1)S(1)} collective-permute-done((bf16[7,24,384]{2,1,0:T(8,128)(2,1)S(1)}, bf16[7,24,384]{2,1,0:T(8,128)(2,1)S(1)}, u32[]{:S(2)}, u32[]{:S(2)}) %collective-permute-start) | collective-permute-done | bytes 129056 | tf_op jit(solution)/shard_map/ppermute | solution.py:373
  2.4 0.0 copy-done.5
  2.4 0.0 copy-start
  2.5 0.0 copy-start.1
  2.5 0.0 copy-start.2
  2.5 0.0 copy-start.3
  2.5 0.0 copy-start.4
  2.6 0.9 %copy-done = bf16[27,16,384]{2,1,0:T(8,128)(2,1)S(1)} copy-done((bf16[27,16,384]{2,1,0:T(8,128)(2,1)S(1)}, bf16[27,16,384]{2,1,0:T(8,128)(2,1)}, u32[]{:S(2)}) %copy-start) | copy-done | bytes 331800
  3.4 0.0 copy-done.1
  3.4 0.0 copy-done.2
  3.4 0.0 copy-done.3
  3.4 0.0 copy-done.4
  3.4 42.4 %shard_map.73 = bf16[384,384]{1,0:T(8,128)(2,1)S(1)} custom-call(bf16[4,16,128]{2,1,0:T(8,128)(2,1)S(1)} %pad.8.latq, s32[8]{0:T(128)S(1)} %copy-done.4, bf16[432,384]{1,0:T(8,128)(2,1)S(1)} %bitcast.13, f32[384]{0:T(512)S(1)} %copy-done.1, f32[384]{0:T(512)S(1)} %copy-done.2, f32[384]{0:T(512)S(1)} %copy-done.3, ...), custom_call_target="tpu_custom_call" | custom-call | flops 5000000000 | bytes 2000000 | tf_op jit(solution)/shard_map/pallas_call | solution.py:384
  45.8 0.7 %copy.14 = bf16[4,6,16,384]{3,2,1,0:T(8,128)(2,1)} copy(bf16[4,6,16,384]{3,2,1,0:T(8,128)(2,1)S(1)} %bitcast.12) | data formatting | bytes 589824
  (4 shorter events, 0.1 us)
Async XLA Ops:
  0.0 2.4 %copy-start.5 = (bf16[27,24,384]{2,1,0:T(8,128)(2,1)S(1)}, bf16[27,24,384]{2,1,0:T(8,128)(2,1)}, u32[]{:S(2)}) copy-start(bf16[27,24,384]{2,1,0:T(8,128)(2,1)} %param.12) | copy-start | bytes 1492996
  0.0 1.1 %copy-start.6 = (bf16[16,384]{1,0:T(8,128)(2,1)S(1)}, bf16[16,384]{1,0:T(8,128)(2,1)}, u32[]{:S(2)}) copy-start(bf16[16,384]{1,0:T(8,128)(2,1)} %param.7) | copy-start | bytes 36868
  1.0 1.4 %collective-permute-start = (bf16[7,24,384]{2,1,0:T(8,128)(2,1)S(1)}, bf16[7,24,384]{2,1,0:T(8,128)(2,1)S(1)}, u32[]{:S(2)}, u32[]{:S(2)}) collective-permute-start(bf16[7,24,384]{2,1,0:T(8,128)(2,1)S(1)} %pad_dynamic-slice_fusion), channel_id=1, source_target_pairs={{0,1},{1,0},{2,3},{3,2},{4,5},{5,4},{6,7},{7,6},{8,9},{9,8},{10,11... | collective-permute-start | bytes 387080 | tf_op jit(solution)/shard_map/ppermute | solution.py:373
  2.4 1.0 %copy-start = (bf16[27,16,384]{2,1,0:T(8,128)(2,1)S(1)}, bf16[27,16,384]{2,1,0:T(8,128)(2,1)}, u32[]{:S(2)}) copy-start(bf16[27,16,384]{2,1,0:T(8,128)(2,1)} %param.9) | copy-start | bytes 995332
  2.5 1.0 %copy-start.1 = (f32[384]{0:T(512)S(1)}, f32[384]{0:T(512)}, u32[]{:S(2)}) copy-start(f32[384]{0:T(512)} %entry_bias_far.1) | copy-start | bytes 4612
  2.5 1.0 %copy-start.2 = (f32[384]{0:T(512)S(1)}, f32[384]{0:T(512)}, u32[]{:S(2)}) copy-start(f32[384]{0:T(512)} %gain_far.1) | copy-start | bytes 4612
  2.5 0.9 %copy-start.3 = (f32[384]{0:T(512)S(1)}, f32[384]{0:T(512)}, u32[]{:S(2)}) copy-start(f32[384]{0:T(512)} %residual_bias_far.1) | copy-start | bytes 4612
  2.5 0.9 %copy-start.4 = (s32[8]{0:T(128)S(1)}, s32[8]{0:T(128)}, u32[]{:S(2)}) copy-start(s32[8]{0:T(128)} %counts.1) | copy-start | bytes 100
where the time goes:
time: 46.7 us; the launch traced here: 46.5 us
  Pallas kernels  42.4 us (91%)
  local copies, waits for them, and re-layouts  2.7 us (6%)
  waiting for transfers between devices  1.19 us (3%)
    pallas_call x1, Pallas kernels, sliced_shards(): pl.pallas_call(section_kernel, out_shape=jax.ShapeDtypeStruct((4 * CELLS,...  42.4 us
    unnamed x15, local copies, waits for them, and re-layouts  1.62 us
    ppermute x1, waiting for transfers between devices, sliced_shards(): received = lax.ppermute(theirs, 'tm', [(i, i ^ 1) for i in range(16)])  1.19 us
    dynamic_slice x1, local copies, waits for them, and re-layouts, sliced_shards(): theirs = lax.dynamic_slice_in_dim(quarters, (2 * x + 1 - c) * TAPS, TAPS, 0)  0.98 us
  transfers between devices with their start and end apart: 1, of which 1 were waited for; matrix products, arithmetic and copies ran while one was open for 0% of the time, Pallas kernels for 0%

commit v1 on v0

v1 whole, which is shorter than its diff:
```python
import jax
import jax.numpy as jnp
from jax import lax
from jax.experimental import pallas as pl
from jax.experimental.pallas import tpu as pltpu
from jax.sharding import PartitionSpec as P

LATENT_CHANNELS = 16
C = 384
PROMPT_SAMPLES = 8
BLOCK_FRAMES = 4
LATENT_ROWS = 6
LATENT_COLUMNS = 16


def from_behind(block, axis, distance):
    devices = range(lax.axis_size(axis))
    route = [(i - distance, i) for i in devices if i - distance in devices]
    return lax.ppermute(block, axis, route)


def causal_conv(frames, weight):
    frames_out = frames.shape[0] - 2
    inputs = frames.shape[3]
    padded = jnp.pad(frames, ((0, 0), (1, 1), (1, 1), (0, 0)))
    total = jnp.zeros((frames_out * LATENT_ROWS * LATENT_COLUMNS, weight.shape[2]), jnp.float32)
    for time_tap in range(3):
        for row_tap in range(3):
            for col_tap in range(3):
                window = padded[
                    time_tap : time_tap + frames_out,
                    row_tap : row_tap + LATENT_ROWS,
                    col_tap : col_tap + LATENT_COLUMNS,
                    :,
                ]
                window = window.reshape(frames_out * LATENT_ROWS * LATENT_COLUMNS, inputs)
                tap = 9 * time_tap + 3 * row_tap + col_tap
                total = total + jnp.dot(window, weight[tap], preferred_element_type=jnp.float32)
    return total


def activate(stream, norm_scale_gain):
    values = stream.astype(jnp.float32)
    scale = lax.rsqrt(jnp.mean(values * values, axis=-1, keepdims=True) + 1e-06)
    return jax.nn.silu(values * scale * norm_scale_gain).astype(jnp.bfloat16)


def to_cells(planes):
    return jnp.transpose(
        planes.reshape(planes.shape[0], LATENT_CHANNELS, LATENT_ROWS, LATENT_COLUMNS), (0, 2, 3, 1)
    )


def shards(
    sharded_latents,
    sample_frame_count,
    entry_kernel,
    entry_bias,
    norm_scale_gain,
    residual_kernel,
    residual_bias,
):
    gathered_latents = lax.all_to_all(
        sharded_latents, "tm", split_axis=0, concat_axis=1, tiled=True
    )
    latent_volume = gathered_latents.reshape(
        BLOCK_FRAMES, LATENT_CHANNELS, LATENT_ROWS * LATENT_COLUMNS
    )
    position = lax.axis_index("tm")
    block = position // PROMPT_SAMPLES
    sample = position % PROMPT_SAMPLES
    keep = block > 0
    earlier = from_behind(latent_volume, "tm", PROMPT_SAMPLES)
    earlier = jnp.where(keep, earlier, jnp.zeros_like(earlier))
    frames = to_cells(jnp.concatenate([earlier, latent_volume], axis=0))
    widened = (causal_conv(frames, entry_kernel) + entry_bias).astype(jnp.bfloat16)
    active_all = activate(widened, norm_scale_gain).reshape(
        BLOCK_FRAMES + 2, LATENT_ROWS, LATENT_COLUMNS, C
    )
    behind = jnp.where(keep, active_all[:2], jnp.zeros_like(active_all[:2]))
    extended = jnp.concatenate([behind, active_all[2:]], axis=0)
    stream = widened[2 * LATENT_ROWS * LATENT_COLUMNS :]
    kernel_all = lax.all_gather(residual_kernel, "tm", axis=1, tiled=True)
    branch = causal_conv(extended, kernel_all)
    total = (stream.astype(jnp.float32) + (branch + residual_bias)).reshape(
        BLOCK_FRAMES, LATENT_ROWS, LATENT_COLUMNS, C
    )
    limit = jnp.sum(jnp.where(jnp.arange(PROMPT_SAMPLES) == sample, sample_frame_count, 0))
    frame_index = block * BLOCK_FRAMES + jnp.arange(BLOCK_FRAMES)
    valid = (frame_index < limit)[:, None, None, None]
    return jnp.where(valid, total, jnp.zeros_like(total)).astype(jnp.bfloat16)


MESH = pl.DeviceIdType.MESH
F32, BF16 = jnp.float32, jnp.bfloat16
CELLS = LATENT_ROWS * LATENT_COLUMNS
PLANE = 128
SLICES = 3
CHUNKS = ((0, 8, 12, 7), (8, 3, 6, 3), (11, 3, 0, 3))
LOCAL_TAPS = 14


def place_of(tap):
    if tap >= 12:
        return (0, tap - 12) if tap < 20 else (1, tap - 19)
    if tap >= 6:
        return (tap - 6) // 3, 8 + tap % 3
    return tap // 3, 11 + tap % 3


def section_kernel(
    latq, counts, entry_far, entry_bias_far, gain_far, residual_bias_far, taps_far,
    out,
    entry, entry_bias, gain, residual_bias, lat, at, act, kept, blocks, right, acc, done,
    lat_send, lat_recv, z_send, z_recv, y_send, y_recv, x_send, x_recv, r_send, r_recv,
    d_send, d_recv, c_send, c_recv, o_send, o_recv, own,
):
    x = lax.axis_index("groups")
    me = lax.axis_index("tm")
    z, y, c = me // 4, (me // 2) % 2, me % 2

    def where_(zz, yy, cc):
        return {"tm": zz * 4 + yy * 2 + cc}

    row_peer = {"groups": x, "tm": z * 4 + (1 - y) * 2 + c}
    col_peer = {"groups": 1 - x, "tm": me}
    far_peer = {"groups": 1 - x, "tm": z * 4 + (1 - y) * 2 + c}
    sibling = {"tm": z * 4 + y * 2 + (1 - c)}

    barrier = pltpu.get_barrier_semaphore()
    for step in range(1, 16):
        pl.semaphore_signal(barrier, inc=1, device_id={"tm": lax.rem(me + step, 16)}, device_id_type=MESH)
    for peer in (col_peer, far_peer):
        pl.semaphore_signal(barrier, inc=1, device_id=peer, device_id_type=MESH)
    pl.semaphore_wait(barrier, 17)

    def remote(src, dst, send, recv, device):
        return pltpu.make_async_remote_copy(
            src_ref=src, dst_ref=dst, send_sem=send, recv_sem=recv, device_id=device, device_id_type=MESH
        )

    def columns(n):
        return pl.ds(pl.multiple_of(128 * n, 128), 128)

    def raw(part, ch, n):
        _, count, first, step = CHUNKS[ch]
        return taps_far.at[pl.ds(first + step * part, count), :, columns(n)]

    def block(part, ch, zz, yy, cc):
        low, count, _, _ = CHUNKS[ch]
        return blocks.at[part, pl.ds(low, count), zz * 4 + yy * 2 + cc]

    def lat_copy(to):
        return remote(latq.at[to % 4], lat.at[me], lat_send.at[to], lat_recv.at[me], {"tm": to})

    def z_copy(ch, n):
        return remote(raw(x, ch, n), block(x, ch, z, y, c), z_send.at[ch, n], z_recv.at[ch, z], where_(n, y, c))

    def z_arrival(ch, zz):
        b = block(x, ch, zz, y, c)
        return remote(b, b, z_send.at[ch, 0], z_recv.at[ch, zz], where_(zz, y, c))

    def y_copy(ch, zz, part=None, source=None):
        at_ = zz if part is None else 4
        b = block(x if part is None else part, ch, zz, y, c)
        return remote(b if source is None else source, b, y_send.at[ch, at_], y_recv.at[ch, at_], row_peer)

    def y_arrival(ch, zz, part=None):
        at_ = zz if part is None else 4
        b = block(x if part is None else part, ch, zz, 1 - y, c)
        return remote(b, b, y_send.at[ch, at_], y_recv.at[ch, at_], row_peer)

    def x_copy(ch, zz):
        b = block(x, ch, zz, y, c)
        return remote(b, b, x_send.at[ch, zz], x_recv.at[ch, zz], col_peer)

    def x_arrival(ch, zz):
        b = block(1 - x, ch, zz, y, c)
        return remote(b, b, x_send.at[ch, zz], x_recv.at[ch, zz], col_peer)

    def r_copy(zz):
        b = block(x, 0, zz, 1 - y, c)
        return remote(b, b, r_send.at[zz], r_recv.at[zz], col_peer)

    def r_arrival(zz):
        b = block(1 - x, 0, zz, 1 - y, c)
        return remote(b, b, r_send.at[zz], r_recv.at[zz], col_peer)

    def d_copy(ch, zz):
        b = block(x, ch, zz, y, c)
        return remote(b, b, d_send.at[ch - 1, zz], d_recv.at[ch - 1, zz], far_peer)

    def d_arrival(ch, zz):
        b = block(1 - x, ch, zz, 1 - y, c)
        return remote(b, b, d_send.at[ch - 1, zz], d_recv.at[ch - 1, zz], far_peer)

    def c_copy(ch, part, zz, yy, source=None):
        b = block(part, ch, zz, yy, c)
        return remote(
            b if source is None else source, b, c_send.at[ch, part, zz, yy], c_recv.at[ch, part, zz, yy], sibling
        )

    def c_arrival(ch, part, zz, yy):
        b = block(part, ch, zz, yy, 1 - c)
        return remote(b, b, c_send.at[ch, part, zz, yy], c_recv.at[ch, part, zz, yy], sibling)

    def o_copy(d):
        return remote(done.at[d], out.at[:, columns(z)], o_send.at[d], o_recv.at[z], where_(d, y, c))

    def o_arrival(n):
        return remote(done.at[0], out.at[:, columns(n)], o_send.at[0], o_recv.at[n], where_(n, y, c))

    for to in range(12):
        @pl.when(to != me)
        def _():
            lat_copy(to).start()

    for ch in range(3):
        for n in range(SLICES):
            @pl.when(n != z)
            def _():
                z_copy(ch, n).start()

    @pl.when(z < SLICES)
    def _():
        for ch in range(3):
            y_copy(ch, z, None, raw(x, ch, z)).start()
            y_copy(ch, z, 1 - x, raw(1 - x, ch, z)).start()
        for ch in range(3):
            for part in range(2):
                c_copy(ch, part, z, y, raw(part, ch, z)).start()
        mine = [
            pltpu.make_async_copy(latq.at[me % 4], lat.at[me], own.at[0]),
            pltpu.make_async_copy(entry_far, entry, own.at[1]),
            pltpu.make_async_copy(entry_bias_far, entry_bias, own.at[2]),
            pltpu.make_async_copy(gain_far, gain, own.at[3]),
            pltpu.make_async_copy(residual_bias_far, residual_bias, own.at[4]),
        ]
        for ch in range(3):
            for part in range(2):
                mine.append(
                    pltpu.make_async_copy(raw(part, ch, z), block(part, ch, z, y, c), own.at[5 + 2 * ch + part])
                )
        for copy in mine:
            copy.start()

        def near(step):
            at_ = jnp.where(z == 2, 3 - step, step + jnp.where(step >= z, 1, 0))
            at_ = jnp.where((z == 2) & (step == 0), 3, at_)
            return jnp.where((z == 2) & (step > 0), 2 - step, at_)

        def forward(ch, step):
            zz = near(step)
            z_arrival(ch, zz).wait_recv()
            y_copy(ch, zz).start()
            x_copy(ch, zz).start()
            if ch:
                d_copy(ch, zz).start()
            c_copy(ch, x, zz, y).start()

        def from_row_peer(ch):
            y_arrival(ch, z).wait_recv()
            c_copy(ch, x, z, 1 - y).start()
            y_arrival(ch, z, 1 - x).wait_recv()
            c_copy(ch, 1 - x, z, 1 - y).start()
            for step in range(3):
                zz = near(step)
                y_arrival(ch, zz).wait_recv()
                if ch == 0:
                    r_copy(zz).start()
                c_copy(ch, x, zz, 1 - y).start()

        def from_col_peer(ch):
            for step in range(3):
                zz = near(step)
                x_arrival(ch, zz).wait_recv()
                c_copy(ch, 1 - x, zz, y).start()
            for step in range(3):
                zz = near(step)
                if ch == 0:
                    r_arrival(zz).wait_recv()
                else:
                    d_arrival(ch, zz).wait_recv()
                c_copy(ch, 1 - x, zz, 1 - y).start()

        def from_sibling(ch):
            for part in range(2):
                for yy in range(2):
                    for zz in range(4):
                        c_arrival(ch, part, zz, yy).wait_recv()

        at[:, 0:2] = jnp.zeros((2, 2, 144, PLANE), BF16)
        acc[...] = jnp.zeros((2, 10, PLANE, 128), F32)
        for copy in mine[:5]:
            copy.wait()
        for source in range(16):
            @pl.when(source != me)
            def _():
                remote(latq.at[0], lat.at[source], lat_send.at[0], lat_recv.at[source], {"tm": source}).wait_recv()
        forward(0, 0)
        target = lax.broadcasted_iota(jnp.int32, (256, 256), 0)
        origin = lax.broadcasted_iota(jnp.int32, (256, 256), 1)
        h_, b_, g_, ch_ = target // 128, (target // 64) % 2, (target // 16) % 4, target % 16
        perm = (origin == (g_ * 4 + ch_ // 4) * 16 + (b_ * 2 + h_) * 4 + ch_ % 4).astype(F32).astype(BF16)
        cells = jnp.dot(perm, lat[...].reshape(256, PLANE), preferred_element_type=F32)
        lane = lax.broadcasted_iota(jnp.int32, (256, PLANE), 1)
        row, column = lane // LATENT_COLUMNS, lane % LATENT_COLUMNS
        for j in range(3):
            for k in range(3):
                offset = (j - 1) * LATENT_COLUMNS + (k - 1)
                moved = pltpu.roll(cells, (-offset) % PLANE, 1) if offset else cells
                good = (
                    (row + (j - 1) >= 0)
                    & (row + (j - 1) < LATENT_ROWS)
                    & (column + (k - 1) >= 0)
                    & (column + (k - 1) < LATENT_COLUMNS)
                )
                tap = 3 * j + k
                at[:, 2:, tap * 16 : tap * 16 + 16, :] = (
                    jnp.where(good, moved, 0.0).astype(BF16).reshape(2, 8, 16, PLANE)
                )

        def inlet(index):
            h, b = index // 2, index % 2
            left = jnp.concatenate([at[h, 4 * b + q : 4 * b + q + 3].reshape(432, PLANE) for q in range(4)], axis=1)
            wide = lax.dot_general(left, entry[...], (((0,), (0,)), ((), ())), preferred_element_type=F32)
            wide = wide.reshape(4, PLANE, C)[:, :CELLS].reshape(4 * CELLS, C)
            stream = (wide + entry_bias[...][None, :]).astype(BF16)
            kept[4 * index : 4 * index + 4] = stream.reshape(4, CELLS, C)
            values = stream.astype(F32)
            scale = lax.rsqrt(jnp.mean(values * values, axis=-1, keepdims=True) + 1e-06)
            u = values * scale * gain[...][None, :]
            active = (u / (1.0 + jnp.exp(-u))).astype(BF16).astype(F32)
            column = lax.broadcasted_iota(jnp.int32, (4 * CELLS, C), 0) % LATENT_COLUMNS
            rows = slice(4 * b, 4 * b + 4)
            before = jnp.where(column == 0, 0.0, pltpu.roll(active, 1, 0))
            behind = jnp.where(column == LATENT_COLUMNS - 1, 0.0, pltpu.roll(active, 4 * CELLS - 1, 0))
            for k, moved in enumerate((before, active, behind)):
                act[h, rows, :, k * C : k * C + C] = moved.astype(BF16).reshape(4, CELLS, C)

        def prepare(low, high):
            for tap in range(low, high):
                part, local = place_of(tap)
                slot, k = tap // 3, tap % 3
                index = 8 - slot + (1 if slot < 4 else 0)
                piece = blocks[part, local].astype(F32).reshape(C, 128).astype(BF16)
                right[index // 2, k * C : k * C + C, index % 2 * 128 : index % 2 * 128 + 128] = piece

        def sweep(h, tile, slots, frames):
            left = act[h, :frames].reshape(frames * CELLS, 3 * C)
            wide = jnp.dot(left, right[tile, :, : 128 * len(slots)], preferred_element_type=F32)
            for n, slot in enumerate(slots):
                i, j = slot // 3, slot % 3
                part = wide[:, 128 * n : 128 * n + 128].reshape(frames, CELLS, 128)
                acc[h, 2 - i : 2 - i + frames, 16 * (2 - j) : 16 * (2 - j) + CELLS] += part

        inlet(0)
        forward(0, 1)
        forward(0, 2)
        inlet(1)
        for step in range(3):
            forward(1, step)
        from_row_peer(0)
        inlet(2)
        for step in range(3):
            forward(2, step)
        inlet(3)
        from_col_peer(0)
        for copy in mine[5:]:
            copy.wait()
        from_row_peer(1)
        from_sibling(0)
        prepare(12, 27)

        def first(h, carry):
            sweep(h, 0, (8, 7), 8)
            sweep(h, 1, (6, 5), 8)
            sweep(h, 2, (4,), 7)
            return carry

        lax.fori_loop(0, 1, first, 0)
        from_col_peer(1)
        from_row_peer(2)
        lax.fori_loop(1, 2, first, 0)
        from_col_peer(2)
        from_sibling(1)
        prepare(6, 12)

        def second(h, carry):
            sweep(h, 3, (3, 2), 7)
            return carry

        lax.fori_loop(0, 2, second, 0)
        from_sibling(2)
        prepare(0, 6)

        def finish(step, carry):
            h = 1 - step
            sweep(h, 4, (1, 0), 6)
            for b in (1, 0):
                d = 2 * b + h
                stream = kept[pl.ds(h * 8 + b * 4, 4), :, columns(z)].astype(F32)
                total = acc[h, 4 * b : 4 * b + 4, 16 : 16 + CELLS] + residual_bias[columns(z)][None, None, :]
                total = stream + total
                limit = counts[me % 4 + 4 * h]
                valid = lax.broadcasted_iota(jnp.int32, (4, CELLS, 128), 0) + 4 * b < limit
                done[d] = jnp.where(valid, total, 0.0).astype(BF16).reshape(4 * CELLS, 128)

                @pl.when(d != z)
                def _():
                    o_copy(d).start()

            return carry

        lax.fori_loop(0, 2, finish, 0)
        out[:, columns(z)] = done[z]

    for n in range(SLICES):
        @pl.when(n != z)
        def _():
            o_arrival(n).wait_recv()
            for ch in range(3):
                z_copy(ch, n).wait_send()

    for to in range(12):
        @pl.when(to != me)
        def _():
            lat_copy(to).wait_send()

    @pl.when(z < SLICES)
    def _():
        for ch in range(3):
            y_copy(ch, z, 1 - x).wait_send()
            for zz in range(4):
                y_copy(ch, zz).wait_send()

                @pl.when(zz != z)
                def _():
                    x_copy(ch, zz).wait_send()
                    if ch == 0:
                        r_copy(zz).wait_send()
                    else:
                        d_copy(ch, zz).wait_send()

                for part in range(2):
                    for yy in range(2):
                        c_copy(ch, part, zz, yy).wait_send()
        for d in range(4):
            @pl.when(d != z)
            def _():
                o_copy(d).wait_send()


def sliced_shards(
    sharded_latents,
    sample_frame_count,
    entry_kernel,
    entry_bias,
    norm_scale_gain,
    residual_kernel,
    residual_bias,
):
    latq = jnp.transpose(sharded_latents.reshape(4, 4, 4, CELLS), (1, 0, 2, 3)).reshape(4, 16, CELLS)
    latq = jnp.pad(latq, ((0, 0), (0, 0), (0, PLANE - CELLS)))
    vmem = pl.BlockSpec(memory_space=pltpu.VMEM)
    far = pl.BlockSpec(memory_space=pltpu.HBM)
    dma = pltpu.SemaphoreType.DMA
    out = pl.pallas_call(
        section_kernel,
        out_shape=jax.ShapeDtypeStruct((4 * CELLS, C), BF16),
        in_specs=[vmem, pl.BlockSpec(memory_space=pltpu.SMEM)] + [far] * 5,
        out_specs=vmem,
        scratch_shapes=[
            pltpu.VMEM((27 * LATENT_CHANNELS, C), BF16),
            pltpu.VMEM((C,), F32), pltpu.VMEM((C,), F32), pltpu.VMEM((C,), F32),
            pltpu.VMEM((16, 16, PLANE), BF16),
            pltpu.VMEM((2, 10, 144, PLANE), BF16),
            pltpu.VMEM((2, 8, CELLS, 3 * C), BF16),
            pltpu.VMEM((16, CELLS, C), BF16),
            pltpu.VMEM((2, LOCAL_TAPS, 16, 24, 128), BF16),
            pltpu.VMEM((5, 3 * C, 256), BF16),
            pltpu.VMEM((2, 10, PLANE, 128), F32),
            pltpu.VMEM((4, 4 * CELLS, 128), BF16),
            dma((12,)), dma((16,)), dma((3, 3)), dma((3, 4)), dma((3, 5)), dma((3, 5)),
            dma((3, 4)), dma((3, 4)), dma((4,)), dma((4,)), dma((2, 4)), dma((2, 4)),
            dma((3, 2, 4, 2)), dma((3, 2, 4, 2)), dma((4,)), dma((3,)), dma((11,)),
        ],
        compiler_params=pltpu.CompilerParams(
            collective_id=0, has_side_effects=True, vmem_limit_bytes=56 * 1024 * 1024
        ),
        cost_estimate=pl.CostEstimate(flops=5_000_000_000, bytes_accessed=2_000_000, transcendentals=600_000),
    )(
        latq,
        sample_frame_count,
        entry_kernel.reshape(27 * LATENT_CHANNELS, C),
        entry_bias,
        norm_scale_gain,
        residual_bias,
        residual_kernel,
    )
    return out.reshape(4, LATENT_ROWS, LATENT_COLUMNS, C)


def solution(mesh):
    in_specs = (P("groups", "tm"), P("groups"), P(), P(), P(), P(None, "tm", None), P())
    out_specs = P(("groups", "tm"), None, None, None)
    sliced = mesh.shape["groups"] == 2 and mesh.shape["tm"] == 16
    body = sliced_shards if sliced else shards
    return jax.shard_map(body, mesh=mesh, in_specs=in_specs, out_specs=out_specs, check_vma=False)
```

time: 46.7 us -> 46.7 us (level)
  the two profiles are of different devices: /device:TPU:18 before, /device:TPU:0 now
where the time goes in v1:
time: 46.7 us; the launch traced here: 46.3 us
  Pallas kernels  43.2 us (93%)
  local copies, waits for them, and re-layouts  3.12 us (7%)
    pallas_call x1, Pallas kernels, sliced_shards(): pl.pallas_call(section_kernel, out_shape=jax.ShapeDtypeStruct((4 * CELLS,...  43.2 us
    unnamed x1, local copies, waits for them, and re-layouts  1.71 us

profile of v1, /device:TPU:0, one launch (start us, length us, event | category | flops | bytes accessed | tf_op | source)
XLA Modules:
  0.0 46.3 jit_solution(17951557004093289307)
XLA Ops:
  0.0 0.8 %reshape.12 = bf16[4,4,4,96]{3,2,1,0:T(4,128)(2,1)S(1)} reshape(bf16[16,384]{1,0:T(8,128)(2,1)} %param.7) | data formatting | bytes 24576 | tf_op jit(solution)/shard_map/reshape | solution.py:463
  0.8 0.6 %pad.4.latq = bf16[4,16,128]{2,1,0:T(8,128)(2,1)} pad(bf16[4,16,96]{2,1,0:T(8,128)(2,1)S(1)} %bitcast.6, bf16[]{:T(256)} %constant.2.clone.1), padding=0_0x0_0x0_32 | pad | bytes 28674 | tf_op jit(solution)/shard_map/jit(_pad)/pad | solution.py:464
  1.4 43.2 %shard_map.73 = bf16[384,384]{1,0:T(8,128)(2,1)} custom-call(bf16[4,16,128]{2,1,0:T(8,128)(2,1)} %pad.4.latq, s32[8]{0:T(128)} %counts.1, bf16[432,384]{1,0:T(8,128)(2,1)} %bitcast.7, f32[384]{0:T(512)} %entry_bias_far.1, f32[384]{0:T(512)} %gain_far.1, f32[384]{0:T(512)} %residual_bias_far.1, bf16[27,24,384]{2,1,0:T(8,128)(2,1)} %taps_far.1), custom_call_target="tpu_custom_call" | custom-call | flops 5000000000 | bytes 2000000 | tf_op jit(solution)/shard_map/pallas_call | solution.py:468
  44.6 1.7 %copy.10 = bf16[4,6,16,384]{3,2,1,0:T(8,128)(2,1)} copy(bf16[4,6,16,384]{3,2,1,0:T(8,128)(2,1)} %bitcast.5) | data formatting | bytes 589824
  (1 shorter events, 0.0 us)

commit v2 on v1

v2 whole, which is shorter than its diff:
```python
import jax
import jax.numpy as jnp
from jax import lax
from jax.experimental import pallas as pl
from jax.experimental.pallas import tpu as pltpu
from jax.sharding import PartitionSpec as P

LATENT_CHANNELS = 16
C = 384
PROMPT_SAMPLES = 8
BLOCK_FRAMES = 4
LATENT_ROWS = 6
LATENT_COLUMNS = 16


def from_behind(block, axis, distance):
    devices = range(lax.axis_size(axis))
    route = [(i - distance, i) for i in devices if i - distance in devices]
    return lax.ppermute(block, axis, route)


def causal_conv(frames, weight):
    frames_out = frames.shape[0] - 2
    inputs = frames.shape[3]
    padded = jnp.pad(frames, ((0, 0), (1, 1), (1, 1), (0, 0)))
    total = jnp.zeros((frames_out * LATENT_ROWS * LATENT_COLUMNS, weight.shape[2]), jnp.float32)
    for time_tap in range(3):
        for row_tap in range(3):
            for col_tap in range(3):
                window = padded[
                    time_tap : time_tap + frames_out,
                    row_tap : row_tap + LATENT_ROWS,
                    col_tap : col_tap + LATENT_COLUMNS,
                    :,
                ]
                window = window.reshape(frames_out * LATENT_ROWS * LATENT_COLUMNS, inputs)
                tap = 9 * time_tap + 3 * row_tap + col_tap
                total = total + jnp.dot(window, weight[tap], preferred_element_type=jnp.float32)
    return total


def activate(stream, norm_scale_gain):
    values = stream.astype(jnp.float32)
    scale = lax.rsqrt(jnp.mean(values * values, axis=-1, keepdims=True) + 1e-06)
    return jax.nn.silu(values * scale * norm_scale_gain).astype(jnp.bfloat16)


def to_cells(planes):
    return jnp.transpose(
        planes.reshape(planes.shape[0], LATENT_CHANNELS, LATENT_ROWS, LATENT_COLUMNS), (0, 2, 3, 1)
    )


def shards(
    sharded_latents,
    sample_frame_count,
    entry_kernel,
    entry_bias,
    norm_scale_gain,
    residual_kernel,
    residual_bias,
):
    gathered_latents = lax.all_to_all(
        sharded_latents, "tm", split_axis=0, concat_axis=1, tiled=True
    )
    latent_volume = gathered_latents.reshape(
        BLOCK_FRAMES, LATENT_CHANNELS, LATENT_ROWS * LATENT_COLUMNS
    )
    position = lax.axis_index("tm")
    block = position // PROMPT_SAMPLES
    sample = position % PROMPT_SAMPLES
    keep = block > 0
    earlier = from_behind(latent_volume, "tm", PROMPT_SAMPLES)
    earlier = jnp.where(keep, earlier, jnp.zeros_like(earlier))
    frames = to_cells(jnp.concatenate([earlier, latent_volume], axis=0))
    widened = (causal_conv(frames, entry_kernel) + entry_bias).astype(jnp.bfloat16)
    active_all = activate(widened, norm_scale_gain).reshape(
        BLOCK_FRAMES + 2, LATENT_ROWS, LATENT_COLUMNS, C
    )
    behind = jnp.where(keep, active_all[:2], jnp.zeros_like(active_all[:2]))
    extended = jnp.concatenate([behind, active_all[2:]], axis=0)
    stream = widened[2 * LATENT_ROWS * LATENT_COLUMNS :]
    kernel_all = lax.all_gather(residual_kernel, "tm", axis=1, tiled=True)
    branch = causal_conv(extended, kernel_all)
    total = (stream.astype(jnp.float32) + (branch + residual_bias)).reshape(
        BLOCK_FRAMES, LATENT_ROWS, LATENT_COLUMNS, C
    )
    limit = jnp.sum(jnp.where(jnp.arange(PROMPT_SAMPLES) == sample, sample_frame_count, 0))
    frame_index = block * BLOCK_FRAMES + jnp.arange(BLOCK_FRAMES)
    valid = (frame_index < limit)[:, None, None, None]
    return jnp.where(valid, total, jnp.zeros_like(total)).astype(jnp.bfloat16)


MESH = pl.DeviceIdType.MESH
F32, BF16 = jnp.float32, jnp.bfloat16
CELLS = LATENT_ROWS * LATENT_COLUMNS
PLANE = 128
HALF = 64
SLICES = 3
PAIRS = ((8, 7), (6, 5), (4, 3), (2, 1), (0, 0))
CHUNKS = ((0, 1), (2, 3), (4,))


def section_kernel(
    lat_far, counts, entry_far, entry_bias_far, gain_far, residual_bias_far, taps_far,
    out,
    entry, entry_bias, gain, residual_bias, lat_raw, taps, latq, lat, at, act, kept,
    piece_a, piece_b, piece_c, block_a, block_b, block_c, right, acc, done, got,
    lat_send, lat_recv, z_send, z_recv, y_send, y_recv, c_send, c_recv, o_send, o_recv, own,
):
    x = lax.axis_index("groups")
    me = lax.axis_index("tm")
    z, y, c = me // 4, (me // 2) % 2, me % 2
    pieces = (piece_a, piece_b, piece_c)
    blocks = (block_a, block_b, block_c)

    barrier = pltpu.get_barrier_semaphore()
    for step in range(1, 16):
        pl.semaphore_signal(barrier, inc=1, device_id={"tm": lax.rem(me + step, 16)}, device_id_type=MESH)
    for step in range(16):
        pl.semaphore_signal(
            barrier, inc=1, device_id={"groups": 1 - x, "tm": lax.rem(me + step, 16)}, device_id_type=MESH
        )

    first_copies = [
        pltpu.make_async_copy(lat_far, lat_raw, own.at[0]),
        pltpu.make_async_copy(taps_far, taps, own.at[1]),
        pltpu.make_async_copy(entry_far, entry, own.at[2]),
        pltpu.make_async_copy(entry_bias_far, entry_bias, own.at[3]),
        pltpu.make_async_copy(gain_far, gain, own.at[4]),
        pltpu.make_async_copy(residual_bias_far, residual_bias, own.at[5]),
    ]
    for copy in first_copies:
        copy.start()
    first_copies[0].wait()
    cell_rows = lat_raw[...].astype(F32)
    quads = [cell_rows[:, CELLS * q : CELLS * q + CELLS] for q in range(4)]
    quads = jnp.concatenate([jnp.concatenate([q, jnp.zeros((16, PLANE - CELLS), F32)], axis=1) for q in quads], axis=0)
    to_ = lax.broadcasted_iota(jnp.int32, (64, 64), 0)
    from_ = lax.broadcasted_iota(jnp.int32, (64, 64), 1)
    pick = from_ == (to_ % 4) * 16 + ((to_ % 16) // 8) * 8 + ((to_ // 4) % 2) * 4 + to_ // 16
    picked = jnp.dot(pick.astype(F32).astype(BF16), quads.astype(BF16), preferred_element_type=F32)
    latq[...] = picked.astype(BF16).reshape(4, 16, PLANE)
    first_copies[1].wait()
    keeps = (lax.broadcasted_iota(jnp.int32, (24, 128), 1) < HALF) == (x == 0)
    for ch, pairs in enumerate(CHUNKS):
        for n, p in enumerate(pairs):
            low, high = PAIRS[p]
            for k in range(3):
                for s in range(SLICES):
                    a = taps[3 * low + k, :, 128 * s : 128 * s + 128].astype(F32)
                    b = taps[3 * high + k, :, 128 * s : 128 * s + 128].astype(F32)
                    still = jnp.where(x == 0, a, b)
                    moved = pltpu.roll(jnp.where(x == 0, b, a), HALF, 1)
                    pieces[ch][s, 3 * n + k] = jnp.where(keeps, still, moved).astype(BF16)
    pl.semaphore_wait(barrier, 31)

    def remote(src, dst, send, recv, device):
        return pltpu.make_async_remote_copy(
            src_ref=src, dst_ref=dst, send_sem=send, recv_sem=recv, device_id=device, device_id_type=MESH
        )

    def columns(n):
        return pl.ds(pl.multiple_of(128 * n, 128), 128)

    def source_of(zz, yy, cc):
        return zz * 4 + yy * 2 + cc

    def lat_copy(g, to):
        return remote(
            latq.at[to % 4], lat.at[x, me], lat_send.at[g, to], lat_recv.at[x, me], {"groups": g, "tm": to}
        )

    def z_copy(ch, n):
        return remote(
            pieces[ch].at[n], blocks[ch].at[me], z_send.at[ch, n], z_recv.at[ch, z], {"tm": source_of(n, y, c)}
        )

    def z_arrival(ch, zz):
        b = blocks[ch].at[source_of(zz, y, c)]
        return remote(b, b, z_send.at[ch, 0], z_recv.at[ch, zz], {"tm": source_of(zz, y, c)})

    def y_copy(ch, zz, source=None):
        b = blocks[ch].at[source_of(zz, y, c)]
        return remote(
            b if source is None else source, b, y_send.at[ch, zz], y_recv.at[ch, zz], {"tm": source_of(z, 1 - y, c)}
        )

    def y_arrival(ch, zz):
        b = blocks[ch].at[source_of(zz, 1 - y, c)]
        return remote(b, b, y_send.at[ch, zz], y_recv.at[ch, zz], {"tm": source_of(z, 1 - y, c)})

    def c_copy(ch, zz, yy, source=None):
        b = blocks[ch].at[source_of(zz, yy, c)]
        return remote(
            b if source is None else source, b, c_send.at[ch, zz, yy], c_recv.at[ch, zz, yy],
            {"tm": source_of(z, y, 1 - c)},
        )

    def c_arrival(ch, zz, yy):
        b = blocks[ch].at[source_of(zz, yy, 1 - c)]
        return remote(b, b, c_send.at[ch, zz, yy], c_recv.at[ch, zz, yy], {"tm": source_of(z, y, 1 - c)})

    def o_copy(g, h, b):
        return remote(
            done.at[g, h, b], got.at[z, x], o_send.at[g, h, b], o_recv.at[z, x],
            {"groups": g, "tm": source_of(2 * b + h, y, c)},
        )

    def o_arrival(n, xx):
        return remote(
            done.at[0, 0, 0], got.at[n, xx], o_send.at[0, 0, 0], o_recv.at[n, xx],
            {"groups": xx, "tm": source_of(n, y, c)},
        )

    for to in range(12):
        for g in range(2):
            @pl.when((to != me) | (g != x))
            def _():
                lat_copy(g, to).start()

    for ch in range(3):
        for n in range(SLICES):
            @pl.when(n != z)
            def _():
                z_copy(ch, n).start()

    @pl.when(z < SLICES)
    def _():
        mine = [pltpu.make_async_copy(latq.at[me % 4], lat.at[x, me], own.at[6])]
        for ch in range(3):
            y_copy(ch, z, pieces[ch].at[z]).start()
            c_copy(ch, z, y, pieces[ch].at[z]).start()
            mine.append(pltpu.make_async_copy(pieces[ch].at[z], blocks[ch].at[me], own.at[7 + ch]))
        for copy in mine:
            copy.start()

        def near(step):
            at_ = jnp.where(z == 2, 3 - step, step + jnp.where(step >= z, 1, 0))
            at_ = jnp.where((z == 2) & (step == 0), 3, at_)
            return jnp.where((z == 2) & (step > 0), 2 - step, at_)

        def forward(ch, step):
            zz = near(step)
            z_arrival(ch, zz).wait_recv()
            y_copy(ch, zz).start()
            c_copy(ch, zz, y).start()

        def from_row_peer(ch):
            y_arrival(ch, z).wait_recv()
            c_copy(ch, z, 1 - y).start()
            for step in range(3):
                zz = near(step)
                y_arrival(ch, zz).wait_recv()
                c_copy(ch, zz, 1 - y).start()

        def from_sibling(ch):
            for yy in range(2):
                for zz in range(4):
                    c_arrival(ch, zz, yy).wait_recv()

        at[:, 0:2] = jnp.zeros((4, 2, 144, PLANE), BF16)

        def clear(n, carry):
            acc[n // 4, n % 4] = jnp.zeros((10, PLANE, 128), F32)
            return carry

        lax.fori_loop(0, 8, clear, 0)
        for copy in first_copies[2:]:
            copy.wait()
        for copy in mine:
            copy.wait()
        for g in range(2):
            for source in range(16):
                @pl.when((source != me) | (g != x))
                def _():
                    remote(
                        latq.at[0], lat.at[g, source], lat_send.at[0, 0], lat_recv.at[g, source],
                        {"groups": g, "tm": source},
                    ).wait_recv()
        forward(0, 0)
        target = lax.broadcasted_iota(jnp.int32, (256, 256), 0)
        origin = lax.broadcasted_iota(jnp.int32, (256, 256), 1)
        h_, b_, g_, ch_ = target // 128, (target // 64) % 2, (target // 16) % 4, target % 16
        perm = (origin == (g_ * 4 + ch_ // 4) * 16 + (b_ * 2 + h_) * 4 + ch_ % 4).astype(F32).astype(BF16)
        lane = lax.broadcasted_iota(jnp.int32, (256, PLANE), 1)
        row, column = lane // LATENT_COLUMNS, lane % LATENT_COLUMNS

        def spread(g, carry):
            cells = jnp.dot(perm, lat[g].reshape(256, PLANE), preferred_element_type=F32)
            for j in range(3):
                for k in range(3):
                    offset = (j - 1) * LATENT_COLUMNS + (k - 1)
                    moved = pltpu.roll(cells, (-offset) % PLANE, 1) if offset else cells
                    good = (
                        (row + (j - 1) >= 0)
                        & (row + (j - 1) < LATENT_ROWS)
                        & (column + (k - 1) >= 0)
                        & (column + (k - 1) < LATENT_COLUMNS)
                    )
                    tap = 3 * j + k
                    at[pl.ds(2 * g, 2), 2:, tap * 16 : tap * 16 + 16, :] = (
                        jnp.where(good, moved, 0.0).astype(BF16).reshape(2, 8, 16, PLANE)
                    )
            return carry

        def inlet(index, carry):
            h, b = index // 2, index % 2
            left = jnp.concatenate([at[h, pl.ds(4 * b + q, 3)].reshape(432, PLANE) for q in range(4)], axis=1)
            wide = lax.dot_general(left, entry[...], (((0,), (0,)), ((), ())), preferred_element_type=F32)
            wide = wide.reshape(4, PLANE, C)[:, :CELLS].reshape(4 * CELLS, C)
            stream = (wide + entry_bias[...][None, :]).astype(BF16)
            kept[index] = stream
            values = stream.astype(F32)
            scale = lax.rsqrt(jnp.mean(values * values, axis=-1, keepdims=True) + 1e-06)
            u = values * scale * gain[...][None, :]
            active = (u / (1.0 + jnp.exp(-u))).astype(BF16).astype(F32)
            column = lax.broadcasted_iota(jnp.int32, (4 * CELLS, C), 0) % LATENT_COLUMNS
            before = jnp.where(column == 0, 0.0, pltpu.roll(active, 1, 0))
            behind = jnp.where(column == LATENT_COLUMNS - 1, 0.0, pltpu.roll(active, 4 * CELLS - 1, 0))
            for k, moved in enumerate((before, active, behind)):
                act[h, pl.ds(4 * b, 4), :, k * C : k * C + C] = moved.astype(BF16).reshape(4, CELLS, C)
            return carry

        def prepare(ch):
            for n in range(len(CHUNKS[ch])):
                for k in range(3):
                    piece = blocks[ch][:, 3 * n + k].astype(F32).reshape(C, 128).astype(BF16)
                    right[ch, k * C : k * C + C, n * 128 : n * 128 + 128] = piece

        def sweep(h, ch, frames):
            pairs = CHUNKS[ch]
            left = act[h, :frames].reshape(frames * CELLS, 3 * C)
            wide = jnp.dot(left, right[ch, :, : 128 * len(pairs)], preferred_element_type=F32)
            for n, p in enumerate(pairs):
                part = wide[:, 128 * n : 128 * n + 128].reshape(frames, CELLS, 128)
                for side in range(1 if p == 4 else 2):
                    i, j = PAIRS[p][side] // 3, PAIRS[p][side] % 3
                    acc[side, h, 2 - i : 2 - i + frames, 16 * (2 - j) : 16 * (2 - j) + CELLS] += part

        lax.fori_loop(0, 2, spread, 0)
        lax.fori_loop(0, 2, inlet, 0)
        forward(0, 1)
        forward(0, 2)
        lax.fori_loop(2, 4, inlet, 0)
        for step in range(3):
            forward(1, step)
        from_row_peer(0)
        lax.fori_loop(4, 6, inlet, 0)
        for step in range(3):
            forward(2, step)
        lax.fori_loop(6, 8, inlet, 0)
        from_row_peer(1)
        from_sibling(0)
        prepare(0)

        def first(h, carry):
            sweep(h, 0, 8)
            return carry

        lax.fori_loop(0, 2, first, 0)
        from_row_peer(2)
        lax.fori_loop(2, 4, first, 0)
        from_sibling(1)
        prepare(1)
        from_sibling(2)
        prepare(2)
        edge = lax.broadcasted_iota(jnp.int32, (2, CELLS, 128), 2) < HALF
        bias = residual_bias[columns(z)][None, :]
        bias = jnp.where(x == 0, bias, pltpu.roll(jnp.broadcast_to(bias, (8, 128)), HALF, 1)[:1])

        def finish(step, carry):
            g, h = step % 2, 1 - step // 2
            gh = 2 * g + h
            sweep(gh, 1, 7)
            sweep(gh, 2, 6)
            for b in (1, 0):
                stream = kept[2 * gh + b, :, columns(z)].astype(F32)
                stream = jnp.where(x == 0, stream, pltpu.roll(stream, HALF, 1))
                even = acc[0, gh, 4 * b : 4 * b + 4, 16 : 16 + CELLS].reshape(4 * CELLS, 128)
                odd = acc[1, gh, 4 * b : 4 * b + 4, 16 : 16 + CELLS].reshape(4 * CELLS, 128)
                total = stream + (even + pltpu.roll(odd, HALF, 1) + bias)
                top = total[: 2 * CELLS].reshape(2, CELLS, 128)
                low = pltpu.roll(total[2 * CELLS :], HALF, 1).reshape(2, CELLS, 128)
                done[g, h, b] = jnp.where(edge, top, low).astype(BF16).reshape(2 * CELLS, 128)

                @pl.when((g != x) | (2 * b + h != z))
                def _():
                    o_copy(g, h, b).start()

            return carry

        lax.fori_loop(0, 4, finish, 0)
        got[z, x] = done[x, z % 2, z // 2]

    for n in range(SLICES):
        for xx in range(2):
            @pl.when((n != z) | (xx != x))
            def _():
                o_arrival(n, xx).wait_recv()
    limit = counts[me % PROMPT_SAMPLES]
    frame = lax.broadcasted_iota(jnp.int32, (2, CELLS, 128), 0) + BLOCK_FRAMES * (me // PROMPT_SAMPLES)
    half = lax.broadcasted_iota(jnp.int32, (2, CELLS, 128), 2) < HALF
    for n in range(SLICES):
        near_half = got[n, 0].astype(F32)
        far_half = got[n, 1].astype(F32)
        top = jnp.where(half, near_half.reshape(2, CELLS, 128), pltpu.roll(far_half, HALF, 1).reshape(2, CELLS, 128))
        low = jnp.where(half, pltpu.roll(near_half, HALF, 1).reshape(2, CELLS, 128), far_half.reshape(2, CELLS, 128))
        for first_frame, values in ((0, top), (2, low)):
            values = jnp.where(frame + first_frame < limit, values, 0.0).astype(BF16)
            out[CELLS * first_frame : CELLS * (first_frame + 2), 128 * n : 128 * n + 128] = values.reshape(2 * CELLS, 128)

    @pl.when(z == SLICES)
    def _():
        for copy in first_copies[2:]:
            copy.wait()

    for n in range(SLICES):
        @pl.when(n != z)
        def _():
            for ch in range(3):
                z_copy(ch, n).wait_send()

    for to in range(12):
        for g in range(2):
            @pl.when((to != me) | (g != x))
            def _():
                lat_copy(g, to).wait_send()

    @pl.when(z < SLICES)
    def _():
        for ch in range(3):
            for zz in range(4):
                y_copy(ch, zz).wait_send()
                for yy in range(2):
                    c_copy(ch, zz, yy).wait_send()
        for g in range(2):
            for h in range(2):
                for b in range(2):
                    @pl.when((g != x) | (2 * b + h != z))
                    def _():
                        o_copy(g, h, b).wait_send()


def sliced_shards(
    sharded_latents,
    sample_frame_count,
    entry_kernel,
    entry_bias,
    norm_scale_gain,
    residual_kernel,
    residual_bias,
):
    vmem = pl.BlockSpec(memory_space=pltpu.VMEM)
    far = pl.BlockSpec(memory_space=pltpu.HBM)
    dma = pltpu.SemaphoreType.DMA
    pairs = [3 * len(chunk) for chunk in CHUNKS]
    out = pl.pallas_call(
        section_kernel,
        out_shape=jax.ShapeDtypeStruct((4 * CELLS, C), BF16),
        in_specs=[far, pl.BlockSpec(memory_space=pltpu.SMEM)] + [far] * 5,
        out_specs=vmem,
        scratch_shapes=[
            pltpu.VMEM((27 * LATENT_CHANNELS, C), BF16),
            pltpu.VMEM((C,), F32), pltpu.VMEM((C,), F32), pltpu.VMEM((C,), F32),
            pltpu.VMEM((16, 4 * CELLS), BF16),
            pltpu.VMEM((27, 24, C), BF16),
            pltpu.VMEM((4, 16, PLANE), BF16),
            pltpu.VMEM((2, 16, 16, PLANE), BF16),
            pltpu.VMEM((4, 10, 144, PLANE), BF16),
            pltpu.VMEM((4, 8, CELLS, 3 * C), BF16),
            pltpu.VMEM((8, 4 * CELLS, C), BF16),
        ]
        + [pltpu.VMEM((SLICES, n, 24, 128), BF16) for n in pairs]
        + [pltpu.VMEM((16, n, 24, 128), BF16) for n in pairs]
        + [
            pltpu.VMEM((3, 3 * C, 256), BF16),
            pltpu.VMEM((2, 4, 10, PLANE, 128), F32),
            pltpu.VMEM((2, 2, 2, 2 * CELLS, 128), BF16),
            pltpu.VMEM((SLICES, 2, 2 * CELLS, 128), BF16),
            dma((2, 12)), dma((2, 16)), dma((3, 3)), dma((3, 4)), dma((3, 4)), dma((3, 4)),
            dma((3, 4, 2)), dma((3, 4, 2)), dma((2, 2, 2)), dma((3, 2)), dma((10,)),
        ],
        compiler_params=pltpu.CompilerParams(
            collective_id=0, has_side_effects=True, vmem_limit_bytes=56 * 1024 * 1024
        ),
        cost_estimate=pl.CostEstimate(flops=5_000_000_000, bytes_accessed=2_000_000, transcendentals=600_000),
    )(
        sharded_latents,
        sample_frame_count,
        entry_kernel.reshape(27 * LATENT_CHANNELS, C),
        entry_bias,
        norm_scale_gain,
        residual_bias,
        residual_kernel,
    )
    return out.reshape(4, LATENT_ROWS, LATENT_COLUMNS, C)


def solution(mesh):
    in_specs = (P("groups", "tm"), P("groups"), P(), P(), P(), P(None, "tm", None), P())
    out_specs = P(("groups", "tm"), None, None, None)
    sliced = mesh.shape["groups"] == 2 and mesh.shape["tm"] == 16
    body = sliced_shards if sliced else shards
    return jax.shard_map(body, mesh=mesh, in_specs=in_specs, out_specs=out_specs, check_vma=False)
```

time: 46.7 us -> 40.3 us (0.86)
  the two profiles are of different devices: /device:TPU:0 before, /device:TPU:18 now
where the time goes in v2:
time: 40.3 us; the launch traced here: 39.9 us
  Pallas kernels  38.2 us (95%)
  local copies, waits for them, and re-layouts  1.71 us (4%)
    pallas_call x1, Pallas kernels, sliced_shards(): pl.pallas_call(section_kernel, out_shape=jax.ShapeDtypeStruct((4 * CELLS,...  38.2 us
    unnamed x1, local copies, waits for them, and re-layouts  1.71 us

profile of v2, /device:TPU:18, one launch (start us, length us, event | category | flops | bytes accessed | tf_op | source)
XLA Modules:
  0.0 39.9 jit_solution(3100395567161227420)
XLA Ops:
  0.0 38.2 %shard_map.73 = bf16[384,384]{1,0:T(8,128)(2,1)} custom-call(bf16[16,384]{1,0:T(8,128)(2,1)} %lat_far.1, s32[8]{0:T(128)} %counts.1, bf16[432,384]{1,0:T(8,128)(2,1)} %bitcast.3, f32[384]{0:T(512)} %entry_bias_far.1, f32[384]{0:T(512)} %gain_far.1, f32[384]{0:T(512)} %residual_bias_far.1, bf16[27,24,384]{2,1,0:T(8,128)(2,1)} %taps_far.1), custom_call_target="tpu_custom_call" | custom-call | flops 5000000000 | bytes 2000000 | tf_op jit(solution)/shard_map/pallas_call | solution.py:458
  38.2 1.7 %copy.9 = bf16[4,6,16,384]{3,2,1,0:T(8,128)(2,1)} copy(bf16[4,6,16,384]{3,2,1,0:T(8,128)(2,1)} %bitcast.2) | data formatting | bytes 589824

commit v3 on v2

--- a/solution.py
+++ b/solution.py
@@ -97,7 +97,7 @@
 PLANE = 128
 HALF = 64
 SLICES = 3
-PAIRS = ((8, 7), (6, 5), (4, 3), (2, 1), (0, 0))
+PAIRS = ((8, 7), (6, 5), (4, 3), (2, 1), (0,))
 CHUNKS = ((0, 1), (2, 3), (4,))
 
 
@@ -106,7 +106,7 @@
     out,
     entry, entry_bias, gain, residual_bias, lat_raw, taps, latq, lat, at, act, kept,
     piece_a, piece_b, piece_c, block_a, block_b, block_c, right, acc, done, got,
-    lat_send, lat_recv, z_send, z_recv, y_send, y_recv, c_send, c_recv, o_send, o_recv, own,
+    lat_send, lat_recv, z_send, z_recv, y_send, y_recv, c_send, c_recv, o_send, o_recv, own, late,
 ):
     x = lax.axis_index("groups")
     me = lax.axis_index("tm")
@@ -115,12 +115,15 @@
     blocks = (block_a, block_b, block_c)
 
     barrier = pltpu.get_barrier_semaphore()
-    for step in range(1, 16):
-        pl.semaphore_signal(barrier, inc=1, device_id={"tm": lax.rem(me + step, 16)}, device_id_type=MESH)
-    for step in range(16):
-        pl.semaphore_signal(
-            barrier, inc=1, device_id={"groups": 1 - x, "tm": lax.rem(me + step, 16)}, device_id_type=MESH
-        )
+
+    @pl.when(z < SLICES)
+    def _():
+        for step in range(1, 16):
+            pl.semaphore_signal(barrier, inc=1, device_id={"tm": lax.rem(me + step, 16)}, device_id_type=MESH)
+        for step in range(16):
+            pl.semaphore_signal(
+                barrier, inc=1, device_id={"groups": 1 - x, "tm": lax.rem(me + step, 16)}, device_id_type=MESH
+            )
 
     first_copies = [
         pltpu.make_async_copy(lat_far, lat_raw, own.at[0]),
@@ -141,19 +144,15 @@
     pick = from_ == (to_ % 4) * 16 + ((to_ % 16) // 8) * 8 + ((to_ // 4) % 2) * 4 + to_ // 16
     picked = jnp.dot(pick.astype(F32).astype(BF16), quads.astype(BF16), preferred_element_type=F32)
     latq[...] = picked.astype(BF16).reshape(4, 16, PLANE)
-    first_copies[1].wait()
-    keeps = (lax.broadcasted_iota(jnp.int32, (24, 128), 1) < HALF) == (x == 0)
-    for ch, pairs in enumerate(CHUNKS):
-        for n, p in enumerate(pairs):
-            low, high = PAIRS[p]
-            for k in range(3):
-                for s in range(SLICES):
-                    a = taps[3 * low + k, :, 128 * s : 128 * s + 128].astype(F32)
-                    b = taps[3 * high + k, :, 128 * s : 128 * s + 128].astype(F32)
-                    still = jnp.where(x == 0, a, b)
-                    moved = pltpu.roll(jnp.where(x == 0, b, a), HALF, 1)
-                    pieces[ch][s, 3 * n + k] = jnp.where(keeps, still, moved).astype(BF16)
-    pl.semaphore_wait(barrier, 31)
+    pl.semaphore_wait(barrier, jnp.where(z < SLICES, 23, 24))
+
+    @pl.when(z == SLICES)
+    def _():
+        for g in range(2):
+            for n in range(SLICES):
+                pl.semaphore_signal(
+                    late, inc=1, device_id={"groups": g, "tm": n * 4 + y * 2 + c}, device_id_type=MESH
+                )
 
     def remote(src, dst, send, recv, device):
         return pltpu.make_async_remote_copy(
@@ -166,10 +165,11 @@
     def source_of(zz, yy, cc):
         return zz * 4 + yy * 2 + cc
 
-    def lat_copy(g, to):
-        return remote(
-            latq.at[to % 4], lat.at[x, me], lat_send.at[g, to], lat_recv.at[x, me], {"groups": g, "tm": to}
-        )
+    def lat_copy(to):
+        return remote(latq.at[to % 4], lat.at[x, me], lat_send.at[to], lat_recv.at[me], {"tm": to})
+
+    def group_copy(g):
+        return remote(lat.at[g], lat.at[g], lat_send.at[12], lat_recv.at[16], {"groups": 1 - x, "tm": me})
 
     def z_copy(ch, n):
         return remote(
@@ -214,12 +214,30 @@
         )
 
     for to in range(12):
-        for g in range(2):
-            @pl.when((to != me) | (g != x))
-            def _():
-                lat_copy(g, to).start()
-
-    for ch in range(3):
+        @pl.when(to != me)
+        def _():
+            lat_copy(to).start()
+
+    first_copies[1].wait()
+    keeps = (lax.broadcasted_iota(jnp.int32, (24, 128), 1) < HALF) == (x == 0)
+
+    def halves(low, high, s):
+        a = taps[low, :, 128 * s : 128 * s + 128].astype(F32)
+        b = taps[high, :, 128 * s : 128 * s + 128].astype(F32)
+        still = jnp.where(x == 0, a, b)
+        moved = pltpu.roll(jnp.where(x == 0, b, a), HALF, 1)
+        return jnp.where(keeps, still, moved).astype(BF16)
+
+    for ch, pairs in enumerate(CHUNKS):
+        for s in range(SLICES):
+            if ch == 2:
+                piece_c[s, 0] = halves(0, 1, s)
+                piece_c[s, 1] = halves(2, 2, s)
+            else:
+                for n, p in enumerate(pairs):
+                    low, high = PAIRS[p]
+                    for k in range(3):
+                        pieces[ch][s, 3 * n + k] = halves(3 * low + k, 3 * high + k, s)
         for n in range(SLICES):
             @pl.when(n != z)
             def _():
@@ -235,22 +253,19 @@
         for copy in mine:
             copy.start()
 
-        def near(step):
-            at_ = jnp.where(z == 2, 3 - step, step + jnp.where(step >= z, 1, 0))
-            at_ = jnp.where((z == 2) & (step == 0), 3, at_)
-            return jnp.where((z == 2) & (step > 0), 2 - step, at_)
-
-        def forward(ch, step):
-            zz = near(step)
-            z_arrival(ch, zz).wait_recv()
-            y_copy(ch, zz).start()
-            c_copy(ch, zz, y).start()
-
-        def from_row_peer(ch):
-            y_arrival(ch, z).wait_recv()
-            c_copy(ch, z, 1 - y).start()
-            for step in range(3):
-                zz = near(step)
+        def other(step):
+            return SLICES if step == 2 else step + jnp.where(step >= z, 1, 0)
+
+        def forward(ch, *steps):
+            for step in steps:
+                zz = other(step)
+                z_arrival(ch, zz).wait_recv()
+                y_copy(ch, zz).start()
+                c_copy(ch, zz, y).start()
+
+        def across(ch, *steps):
+            for step in steps:
+                zz = z if step < 0 else other(step)
                 y_arrival(ch, zz).wait_recv()
                 c_copy(ch, zz, 1 - y).start()
 
@@ -270,15 +285,14 @@
             copy.wait()
         for copy in mine:
             copy.wait()
-        for g in range(2):
-            for source in range(16):
-                @pl.when((source != me) | (g != x))
-                def _():
-                    remote(
-                        latq.at[0], lat.at[g, source], lat_send.at[0, 0], lat_recv.at[g, source],
-                        {"groups": g, "tm": source},
-                    ).wait_recv()
-        forward(0, 0)
+        forward(0, 0, 1)
+        for source in range(16):
+            @pl.when(source != me)
+            def _():
+                remote(
+                    latq.at[0], lat.at[x, source], lat_send.at[0], lat_recv.at[source], {"tm": source}
+                ).wait_recv()
+        group_copy(x).start()
         target = lax.broadcasted_iota(jnp.int32, (256, 256), 0)
         origin = lax.broadcasted_iota(jnp.int32, (256, 256), 1)
         h_, b_, g_, ch_ = target // 128, (target // 64) % 2, (target // 16) % 4, target % 16
@@ -286,7 +300,7 @@
         lane = lax.broadcasted_iota(jnp.int32, (256, PLANE), 1)
         row, column = lane // LATENT_COLUMNS, lane % LATENT_COLUMNS
 
-        def spread(g, carry):
+        def spread(g):
             cells = jnp.dot(perm, lat[g].reshape(256, PLANE), preferred_element_type=F32)
             for j in range(3):
                 for k in range(3):
@@ -302,7 +316,6 @@
                     at[pl.ds(2 * g, 2), 2:, tap * 16 : tap * 16 + 16, :] = (
                         jnp.where(good, moved, 0.0).astype(BF16).reshape(2, 8, 16, PLANE)
                     )
-            return carry
 
         def inlet(index, carry):
             h, b = index // 2, index % 2
@@ -313,8 +326,8 @@
             kept[index] = stream
             values = stream.astype(F32)
             scale = lax.rsqrt(jnp.mean(values * values, axis=-1, keepdims=True) + 1e-06)
-            u = values * scale * gain[...][None, :]
-            active = (u / (1.0 + jnp.exp(-u))).astype(BF16).astype(F32)
+            half_u = values * scale * (0.5 * gain[...])[None, :]
+            active = (half_u + half_u * jnp.tanh(half_u)).astype(BF16).astype(F32)
             column = lax.broadcasted_iota(jnp.int32, (4 * CELLS, C), 0) % LATENT_COLUMNS
             before = jnp.where(column == 0, 0.0, pltpu.roll(active, 1, 0))
             behind = jnp.where(column == LATENT_COLUMNS - 1, 0.0, pltpu.roll(active, 4 * CELLS - 1, 0))
@@ -322,6 +335,20 @@
                 act[h, pl.ds(4 * b, 4), :, k * C : k * C + C] = moved.astype(BF16).reshape(4, CELLS, C)
             return carry
 
+        def prepare_last():
+            for n in range(2):
+                piece = block_c[:, n].astype(F32).reshape(C, 128).astype(BF16)
+                right[2, :C, 128 * n : 128 * n + 128] = piece
+
+        def sweep_last(h):
+            left = act[h, :6, :, C : 2 * C].reshape(6 * CELLS, C)
+            wide = jnp.dot(left, right[2, :C], preferred_element_type=F32)
+            column = lax.broadcasted_iota(jnp.int32, (6 * CELLS, 128), 0) % LATENT_COLUMNS
+            before = jnp.where(column == 0, 0.0, pltpu.roll(wide[:, :128], 1, 0))
+            behind = jnp.where(column == LATENT_COLUMNS - 1, 0.0, pltpu.roll(wide[:, 128:], 6 * CELLS - 1, 0))
+            acc[0, h, 2:8, 32 : 32 + CELLS] += (before + behind).reshape(6, CELLS, 128)
+            acc[1, h, 2:8, 32 : 32 + CELLS] += wide[:, :128].reshape(6, CELLS, 128)
+
         def prepare(ch):
             for n in range(len(CHUNKS[ch])):
                 for k in range(3):
@@ -334,23 +361,48 @@
             wide = jnp.dot(left, right[ch, :, : 128 * len(pairs)], preferred_element_type=F32)
             for n, p in enumerate(pairs):
                 part = wide[:, 128 * n : 128 * n + 128].reshape(frames, CELLS, 128)
-                for side in range(1 if p == 4 else 2):
-                    i, j = PAIRS[p][side] // 3, PAIRS[p][side] % 3
+                for side, slot in enumerate(PAIRS[p]):
+                    i, j = slot // 3, slot % 3
                     acc[side, h, 2 - i : 2 - i + frames, 16 * (2 - j) : 16 * (2 - j) + CELLS] += part
 
-        lax.fori_loop(0, 2, spread, 0)
-        lax.fori_loop(0, 2, inlet, 0)
-        forward(0, 1)
-        forward(0, 2)
-        lax.fori_loop(2, 4, inlet, 0)
-        for step in range(3):
-            forward(1, step)
-        from_row_peer(0)
-        lax.fori_loop(4, 6, inlet, 0)
-        for step in range(3):
-            forward(2, step)
-        lax.fori_loop(6, 8, inlet, 0)
-        from_row_peer(1)
+        def both_groups(step, carry):
+            g = jnp.where(step == 0, x, 1 - x)
+
+            @pl.when(step == 1)
+            def _():
+                group_copy(g).wait_recv()
+
+            spread(g)
+
+            @pl.when(step == 0)
+            def _():
+                forward(1, 0, 1)
+
+            lax.fori_loop(4 * g, 4 * g + 2, inlet, 0)
+
+            @pl.when(step == 0)
+            def _():
+                forward(0, 2)
+                across(0, -1, 0, 1)
+                forward(2, 0, 1)
+
+            @pl.when(step == 1)
+            def _():
+                forward(2, 2)
+                across(0, 2)
+                across(2, -1, 0, 1)
+
+            lax.fori_loop(4 * g + 2, 4 * g + 4, inlet, 0)
+
+            @pl.when(step == 0)
+            def _():
+                forward(1, 2)
+                across(1, -1, 0, 1)
+
+            return carry
+
+        lax.fori_loop(0, 2, both_groups, 0)
+        across(1, 2)
         from_sibling(0)
         prepare(0)
 
@@ -359,12 +411,13 @@
             return carry
 
         lax.fori_loop(0, 2, first, 0)
-        from_row_peer(2)
+        across(2, 2)
         lax.fori_loop(2, 4, first, 0)
         from_sibling(1)
         prepare(1)
         from_sibling(2)
-        prepare(2)
+        prepare_last()
+        pl.semaphore_wait(late, 2)
         edge = lax.broadcasted_iota(jnp.int32, (2, CELLS, 128), 2) < HALF
         bias = residual_bias[columns(z)][None, :]
         bias = jnp.where(x == 0, bias, pltpu.roll(jnp.broadcast_to(bias, (8, 128)), HALF, 1)[:1])
@@ -373,7 +426,7 @@
             g, h = step % 2, 1 - step // 2
             gh = 2 * g + h
             sweep(gh, 1, 7)
-            sweep(gh, 2, 6)
+            sweep_last(gh)
             for b in (1, 0):
                 stream = kept[2 * gh + b, :, columns(z)].astype(F32)
                 stream = jnp.where(x == 0, stream, pltpu.roll(stream, HALF, 1))
@@ -422,13 +475,13 @@
                 z_copy(ch, n).wait_send()
 
     for to in range(12):
-        for g in range(2):
-            @pl.when((to != me) | (g != x))
-            def _():
-                lat_copy(g, to).wait_send()
+        @pl.when(to != me)
+        def _():
+            lat_copy(to).wait_send()
 
     @pl.when(z < SLICES)
     def _():
+        group_copy(x).wait_send()
         for ch in range(3):
             for zz in range(4):
                 y_copy(ch, zz).wait_send()
@@ -454,7 +507,7 @@
     vmem = pl.BlockSpec(memory_space=pltpu.VMEM)
     far = pl.BlockSpec(memory_space=pltpu.HBM)
     dma = pltpu.SemaphoreType.DMA
-    pairs = [3 * len(chunk) for chunk in CHUNKS]
+    pairs = (6, 6, 2)
     out = pl.pallas_call(
         section_kernel,
         out_shape=jax.ShapeDtypeStruct((4 * CELLS, C), BF16),
@@ -478,8 +531,8 @@
             pltpu.VMEM((2, 4, 10, PLANE, 128), F32),
             pltpu.VMEM((2, 2, 2, 2 * CELLS, 128), BF16),
             pltpu.VMEM((SLICES, 2, 2 * CELLS, 128), BF16),
-            dma((2, 12)), dma((2, 16)), dma((3, 3)), dma((3, 4)), dma((3, 4)), dma((3, 4)),
-            dma((3, 4, 2)), dma((3, 4, 2)), dma((2, 2, 2)), dma((3, 2)), dma((10,)),
+            dma((13,)), dma((17,)), dma((3, 3)), dma((3, 4)), dma((3, 4)), dma((3, 4)),
+            dma((3, 4, 2)), dma((3, 4, 2)), dma((2, 2, 2)), dma((3, 2)), dma((10,)), pltpu.SemaphoreType.REGULAR,
         ],
         compiler_params=pltpu.CompilerParams(
             collective_id=0, has_side_effects=True, vmem_limit_bytes=56 * 1024 * 1024

time: 40.3 us -> 38.7 us (0.960)
  Pallas kernels: 38.2 us -> 36.7 us
    pallas_call x1, Pallas kernels: 38.2 us -> 36.7 us  [sliced_shards(): pl.pallas_call(section_kernel, out_shape=jax.ShapeDtypeStruct((4 * CELLS,...]
where the time goes in v3:
time: 38.7 us; the launch traced here: 38.5 us
  Pallas kernels  36.7 us (95%)
  local copies, waits for them, and re-layouts  1.71 us (4%)
    pallas_call x1, Pallas kernels, sliced_shards(): pl.pallas_call(section_kernel, out_shape=jax.ShapeDtypeStruct((4 * CELLS,...  36.7 us
    unnamed x1, local copies, waits for them, and re-layouts  1.71 us

profile of v3, /device:TPU:18, one launch (start us, length us, event | category | flops | bytes accessed | tf_op | source)
XLA Modules:
  0.0 38.5 jit_solution(6468971761887210747)
XLA Ops:
  0.0 36.7 %shard_map.73 = bf16[384,384]{1,0:T(8,128)(2,1)} custom-call(bf16[16,384]{1,0:T(8,128)(2,1)} %lat_far.1, s32[8]{0:T(128)} %counts.1, bf16[432,384]{1,0:T(8,128)(2,1)} %bitcast.3, f32[384]{0:T(512)} %entry_bias_far.1, f32[384]{0:T(512)} %gain_far.1, f32[384]{0:T(512)} %residual_bias_far.1, bf16[27,24,384]{2,1,0:T(8,128)(2,1)} %taps_far.1), custom_call_target="tpu_custom_call" | custom-call | flops 5000000000 | bytes 2000000 | tf_op jit(solution)/shard_map/pallas_call | solution.py:511
  36.8 1.7 %copy.9 = bf16[4,6,16,384]{3,2,1,0:T(8,128)(2,1)} copy(bf16[4,6,16,384]{3,2,1,0:T(8,128)(2,1)} %bitcast.2) | data formatting | bytes 589824

commit v4 on v3

--- a/solution.py
+++ b/solution.py
@@ -102,9 +102,9 @@
 
 
 def section_kernel(
-    lat_far, counts, entry_far, entry_bias_far, gain_far, residual_bias_far, taps_far,
+    lat_far, counts_far, entry_far, entry_bias_far, gain_far, residual_bias_far, taps_far,
     out,
-    entry, entry_bias, gain, residual_bias, lat_raw, taps, latq, lat, at, act, kept,
+    counts, entry, entry_bias, gain, residual_bias, lat_raw, taps, latq, lat, at, act, kept,
     piece_a, piece_b, piece_c, block_a, block_b, block_c, right, acc, done, got,
     lat_send, lat_recv, z_send, z_recv, y_send, y_recv, c_send, c_recv, o_send, o_recv, own, late,
 ):
@@ -132,6 +132,7 @@
         pltpu.make_async_copy(entry_bias_far, entry_bias, own.at[3]),
         pltpu.make_async_copy(gain_far, gain, own.at[4]),
         pltpu.make_async_copy(residual_bias_far, residual_bias, own.at[5]),
+        pltpu.make_async_copy(counts_far, counts, own.at[10]),
     ]
     for copy in first_copies:
         copy.start()
@@ -243,12 +244,21 @@
             def _():
                 z_copy(ch, n).start()
 
+        @pl.when(z < SLICES)
+        def _():
+            y_copy(ch, z, pieces[ch].at[z]).start()
+            c_copy(ch, z, y, pieces[ch].at[z]).start()
+
+        if ch < 2:
+            for n in range(SLICES):
+                @pl.when(z == SLICES)
+                def _():
+                    z_copy(ch, n).wait_send()
+
     @pl.when(z < SLICES)
     def _():
         mine = [pltpu.make_async_copy(latq.at[me % 4], lat.at[x, me], own.at[6])]
         for ch in range(3):
-            y_copy(ch, z, pieces[ch].at[z]).start()
-            c_copy(ch, z, y, pieces[ch].at[z]).start()
             mine.append(pltpu.make_async_copy(pieces[ch].at[z], blocks[ch].at[me], own.at[7 + ch]))
         for copy in mine:
             copy.start()
@@ -406,13 +416,12 @@
         from_sibling(0)
         prepare(0)
 
-        def first(h, carry):
-            sweep(h, 0, 8)
+        def first(step, carry):
+            sweep(2 * step + 1, 0, 8)
             return carry
 
-        lax.fori_loop(0, 2, first, 0)
+        lax.fori_loop(0, 1, first, 0)
         across(2, 2)
-        lax.fori_loop(2, 4, first, 0)
         from_sibling(1)
         prepare(1)
         from_sibling(2)
@@ -425,6 +434,11 @@
         def finish(step, carry):
             g, h = step % 2, 1 - step // 2
             gh = 2 * g + h
+
+            @pl.when(step >= 1)
+            def _():
+                sweep(gh, 0, 8)
+
             sweep(gh, 1, 7)
             sweep_last(gh)
             for b in (1, 0):
@@ -451,6 +465,11 @@
             @pl.when((n != z) | (xx != x))
             def _():
                 o_arrival(n, xx).wait_recv()
+    @pl.when(z == SLICES)
+    def _():
+        for copy in first_copies[2:]:
+            copy.wait()
+
     limit = counts[me % PROMPT_SAMPLES]
     frame = lax.broadcasted_iota(jnp.int32, (2, CELLS, 128), 0) + BLOCK_FRAMES * (me // PROMPT_SAMPLES)
     half = lax.broadcasted_iota(jnp.int32, (2, CELLS, 128), 2) < HALF
@@ -463,16 +482,15 @@
             values = jnp.where(frame + first_frame < limit, values, 0.0).astype(BF16)
             out[CELLS * first_frame : CELLS * (first_frame + 2), 128 * n : 128 * n + 128] = values.reshape(2 * CELLS, 128)
 
-    @pl.when(z == SLICES)
-    def _():
-        for copy in first_copies[2:]:
-            copy.wait()
-
     for n in range(SLICES):
         @pl.when(n != z)
         def _():
-            for ch in range(3):
-                z_copy(ch, n).wait_send()
+            z_copy(2, n).wait_send()
+
+            @pl.when(z < SLICES)
+            def _():
+                for ch in range(2):
+                    z_copy(ch, n).wait_send()
 
     for to in range(12):
         @pl.when(to != me)
@@ -511,9 +529,10 @@
     out = pl.pallas_call(
         section_kernel,
         out_shape=jax.ShapeDtypeStruct((4 * CELLS, C), BF16),
-        in_specs=[far, pl.BlockSpec(memory_space=pltpu.SMEM)] + [far] * 5,
+        in_specs=[far] * 7,
         out_specs=vmem,
         scratch_shapes=[
+            pltpu.SMEM((PROMPT_SAMPLES,), jnp.int32),
             pltpu.VMEM((27 * LATENT_CHANNELS, C), BF16),
             pltpu.VMEM((C,), F32), pltpu.VMEM((C,), F32), pltpu.VMEM((C,), F32),
             pltpu.VMEM((16, 4 * CELLS), BF16),
@@ -532,7 +551,7 @@
             pltpu.VMEM((2, 2, 2, 2 * CELLS, 128), BF16),
             pltpu.VMEM((SLICES, 2, 2 * CELLS, 128), BF16),
             dma((13,)), dma((17,)), dma((3, 3)), dma((3, 4)), dma((3, 4)), dma((3, 4)),
-            dma((3, 4, 2)), dma((3, 4, 2)), dma((2, 2, 2)), dma((3, 2)), dma((10,)), pltpu.SemaphoreType.REGULAR,
+            dma((3, 4, 2)), dma((3, 4, 2)), dma((2, 2, 2)), dma((3, 2)), dma((11,)), pltpu.SemaphoreType.REGULAR,
         ],
         compiler_params=pltpu.CompilerParams(
             collective_id=0, has_side_effects=True, vmem_limit_bytes=56 * 1024 * 1024

time: 38.7 us -> 37.2 us (0.961)
  Pallas kernels: 36.7 us -> 35 us
    pallas_call x1, Pallas kernels: 36.7 us -> 35 us  [sliced_shards(): pl.pallas_call(section_kernel, out_shape=jax.ShapeDtypeStruct((4 * CELLS,...]
where the time goes in v4:
time: 37.2 us; the launch traced here: 36.7 us
  Pallas kernels  35 us (94%)
  local copies, waits for them, and re-layouts  1.71 us (5%)
    pallas_call x1, Pallas kernels, sliced_shards(): pl.pallas_call(section_kernel, out_shape=jax.ShapeDtypeStruct((4 * CELLS,...  35 us
    unnamed x1, local copies, waits for them, and re-layouts  1.71 us

profile of v4, /device:TPU:18, one launch (start us, length us, event | category | flops | bytes accessed | tf_op | source)
XLA Modules:
  0.0 36.7 jit_solution(5296699636517376617)
XLA Ops:
  0.0 35.0 %shard_map.73 = bf16[384,384]{1,0:T(8,128)(2,1)} custom-call(bf16[16,384]{1,0:T(8,128)(2,1)} %lat_far.1, s32[8]{0:T(128)} %counts_far.1, bf16[432,384]{1,0:T(8,128)(2,1)} %bitcast.3, f32[384]{0:T(512)} %entry_bias_far.1, f32[384]{0:T(512)} %gain_far.1, f32[384]{0:T(512)} %residual_bias_far.1, bf16[27,24,384]{2,1,0:T(8,128)(2,1)} %taps_far.1), custom_call_target="tpu_custom_call" | custom-call | flops 5000000000 | bytes 2000000 | tf_op jit(solution)/shard_map/pallas_call | solution.py:529
  35.0 1.7 %copy.9 = bf16[4,6,16,384]{3,2,1,0:T(8,128)(2,1)} copy(bf16[4,6,16,384]{3,2,1,0:T(8,128)(2,1)} %bitcast.2) | data formatting | bytes 589824

commit v5 on v4

--- a/solution.py
+++ b/solution.py
@@ -98,21 +98,21 @@
 HALF = 64
 SLICES = 3
 PAIRS = ((8, 7), (6, 5), (4, 3), (2, 1), (0,))
-CHUNKS = ((0, 1), (2, 3), (4,))
+CHUNKS = ((0, 1), (2, 3))
 
 
 def section_kernel(
     lat_far, counts_far, entry_far, entry_bias_far, gain_far, residual_bias_far, taps_far,
     out,
     counts, entry, entry_bias, gain, residual_bias, lat_raw, taps, latq, lat, at, act, kept,
-    piece_a, piece_b, piece_c, block_a, block_b, block_c, right, acc, done, got,
+    piece_a, piece_b, block_a, block_b, right, acc, done, got,
     lat_send, lat_recv, z_send, z_recv, y_send, y_recv, c_send, c_recv, o_send, o_recv, own, late,
 ):
     x = lax.axis_index("groups")
     me = lax.axis_index("tm")
     z, y, c = me // 4, (me // 2) % 2, me % 2
-    pieces = (piece_a, piece_b, piece_c)
-    blocks = (block_a, block_b, block_c)
+    pieces = (piece_a, piece_b)
+    blocks = (block_a, block_b)
 
     barrier = pltpu.get_barrier_semaphore()
 
@@ -231,14 +231,13 @@
 
     for ch, pairs in enumerate(CHUNKS):
         for s in range(SLICES):
-            if ch == 2:
-                piece_c[s, 0] = halves(0, 1, s)
-                piece_c[s, 1] = halves(2, 2, s)
-            else:
-                for n, p in enumerate(pairs):
-                    low, high = PAIRS[p]
-                    for k in range(3):
-                        pieces[ch][s, 3 * n + k] = halves(3 * low + k, 3 * high + k, s)
+            if ch == 1:
+                piece_b[s, 6] = halves(0, 1, s)
+                piece_b[s, 7] = halves(2, 2, s)
+            for n, p in enumerate(pairs):
+                low, high = PAIRS[p]
+                for k in range(3):
+                    pieces[ch][s, 3 * n + k] = halves(3 * low + k, 3 * high + k, s)
         for n in range(SLICES):
             @pl.when(n != z)
             def _():
@@ -249,7 +248,7 @@
             y_copy(ch, z, pieces[ch].at[z]).start()
             c_copy(ch, z, y, pieces[ch].at[z]).start()
 
-        if ch < 2:
+        if ch < 1:
             for n in range(SLICES):
                 @pl.when(z == SLICES)
                 def _():
@@ -258,7 +257,7 @@
     @pl.when(z < SLICES)
     def _():
         mine = [pltpu.make_async_copy(latq.at[me % 4], lat.at[x, me], own.at[6])]
-        for ch in range(3):
+        for ch in range(2):
             mine.append(pltpu.make_async_copy(pieces[ch].at[z], blocks[ch].at[me], own.at[7 + ch]))
         for copy in mine:
             copy.start()
@@ -347,7 +346,7 @@
 
         def prepare_last():
             for n in range(2):
-                piece = block_c[:, n].astype(F32).reshape(C, 128).astype(BF16)
+                piece = block_b[:, 6 + n].astype(F32).reshape(C, 128).astype(BF16)
                 right[2, :C, 128 * n : 128 * n + 128] = piece
 
         def sweep_last(h):
@@ -394,13 +393,10 @@
             def _():
                 forward(0, 2)
                 across(0, -1, 0, 1)
-                forward(2, 0, 1)
 
             @pl.when(step == 1)
             def _():
-                forward(2, 2)
                 across(0, 2)
-                across(2, -1, 0, 1)
 
             lax.fori_loop(4 * g + 2, 4 * g + 4, inlet, 0)
 
@@ -421,10 +417,8 @@
             return carry
 
         lax.fori_loop(0, 1, first, 0)
-        across(2, 2)
         from_sibling(1)
         prepare(1)
-        from_sibling(2)
         prepare_last()
         pl.semaphore_wait(late, 2)
         edge = lax.broadcasted_iota(jnp.int32, (2, CELLS, 128), 2) < HALF
@@ -485,12 +479,11 @@
     for n in range(SLICES):
         @pl.when(n != z)
         def _():
-            z_copy(2, n).wait_send()
+            z_copy(1, n).wait_send()
 
             @pl.when(z < SLICES)
             def _():
-                for ch in range(2):
-                    z_copy(ch, n).wait_send()
+                z_copy(0, n).wait_send()
 
     for to in range(12):
         @pl.when(to != me)
@@ -500,7 +493,7 @@
     @pl.when(z < SLICES)
     def _():
         group_copy(x).wait_send()
-        for ch in range(3):
+        for ch in range(2):
             for zz in range(4):
                 y_copy(ch, zz).wait_send()
                 for yy in range(2):
@@ -525,7 +518,7 @@
     vmem = pl.BlockSpec(memory_space=pltpu.VMEM)
     far = pl.BlockSpec(memory_space=pltpu.HBM)
     dma = pltpu.SemaphoreType.DMA
-    pairs = (6, 6, 2)
+    pairs = (6, 8)
     out = pl.pallas_call(
         section_kernel,
         out_shape=jax.ShapeDtypeStruct((4 * CELLS, C), BF16),

time: 37.2 us -> 36.9 us (level)
  no operation moved by 1% of the time
where the time goes in v5:
time: 36.9 us; the launch traced here: 36.5 us
  Pallas kernels  34.8 us (94%)
  local copies, waits for them, and re-layouts  1.71 us (5%)
    pallas_call x1, Pallas kernels, sliced_shards(): pl.pallas_call(section_kernel, out_shape=jax.ShapeDtypeStruct((4 * CELLS,...  34.8 us
    unnamed x1, local copies, waits for them, and re-layouts  1.71 us

profile of v5, /device:TPU:18, one launch (start us, length us, event | category | flops | bytes accessed | tf_op | source)
XLA Modules:
  0.0 36.5 jit_solution(2137730398294313807)
XLA Ops:
  0.0 34.8 %shard_map.73 = bf16[384,384]{1,0:T(8,128)(2,1)} custom-call(bf16[16,384]{1,0:T(8,128)(2,1)} %lat_far.1, s32[8]{0:T(128)} %counts_far.1, bf16[432,384]{1,0:T(8,128)(2,1)} %bitcast.3, f32[384]{0:T(512)} %entry_bias_far.1, f32[384]{0:T(512)} %gain_far.1, f32[384]{0:T(512)} %residual_bias_far.1, bf16[27,24,384]{2,1,0:T(8,128)(2,1)} %taps_far.1), custom_call_target="tpu_custom_call" | custom-call | flops 5000000000 | bytes 2000000 | tf_op jit(solution)/shard_map/pallas_call | solution.py:522
  34.8 1.7 %copy.9 = bf16[4,6,16,384]{3,2,1,0:T(8,128)(2,1)} copy(bf16[4,6,16,384]{3,2,1,0:T(8,128)(2,1)} %bitcast.2) | data formatting | bytes 589824

commit v6 on v5

--- a/solution.py
+++ b/solution.py
@@ -397,13 +397,14 @@
             @pl.when(step == 1)
             def _():
                 across(0, 2)
+                across(1, 0, 1)
 
             lax.fori_loop(4 * g + 2, 4 * g + 4, inlet, 0)
 
             @pl.when(step == 0)
             def _():
                 forward(1, 2)
-                across(1, -1, 0, 1)
+                across(1, -1)
 
             return carry
 
@@ -416,7 +417,7 @@
             sweep(2 * step + 1, 0, 8)
             return carry
 
-        lax.fori_loop(0, 1, first, 0)
+        lax.fori_loop(0, 2, first, 0)
         from_sibling(1)
         prepare(1)
         prepare_last()
@@ -429,7 +430,7 @@
             g, h = step % 2, 1 - step // 2
             gh = 2 * g + h
 
-            @pl.when(step >= 1)
+            @pl.when(step >= 2)
             def _():
                 sweep(gh, 0, 8)
 

time: 36.9 us -> 36.7 us (level)
  no operation moved by 1% of the time
where the time goes in v6:
time: 36.7 us; the launch traced here: 36.5 us
  Pallas kernels  34.8 us (95%)
  local copies, waits for them, and re-layouts  1.71 us (5%)
    pallas_call x1, Pallas kernels, sliced_shards(): pl.pallas_call(section_kernel, out_shape=jax.ShapeDtypeStruct((4 * CELLS,...  34.8 us
    unnamed x1, local copies, waits for them, and re-layouts  1.71 us

profile of v6, /device:TPU:18, one launch (start us, length us, event | category | flops | bytes accessed | tf_op | source)
XLA Modules:
  0.0 36.5 jit_solution(6527947131874557430)
XLA Ops:
  0.0 34.8 %shard_map.73 = bf16[384,384]{1,0:T(8,128)(2,1)} custom-call(bf16[16,384]{1,0:T(8,128)(2,1)} %lat_far.1, s32[8]{0:T(128)} %counts_far.1, bf16[432,384]{1,0:T(8,128)(2,1)} %bitcast.3, f32[384]{0:T(512)} %entry_bias_far.1, f32[384]{0:T(512)} %gain_far.1, f32[384]{0:T(512)} %residual_bias_far.1, bf16[27,24,384]{2,1,0:T(8,128)(2,1)} %taps_far.1), custom_call_target="tpu_custom_call" | custom-call | flops 5000000000 | bytes 2000000 | tf_op jit(solution)/shard_map/pallas_call | solution.py:523
  34.8 1.7 %copy.9 = bf16[4,6,16,384]{3,2,1,0:T(8,128)(2,1)} copy(bf16[4,6,16,384]{3,2,1,0:T(8,128)(2,1)} %bitcast.2) | data formatting | bytes 589824

commit v7 on v6

--- a/solution.py
+++ b/solution.py
@@ -294,7 +294,6 @@
             copy.wait()
         for copy in mine:
             copy.wait()
-        forward(0, 0, 1)
         for source in range(16):
             @pl.when(source != me)
             def _():
@@ -302,6 +301,7 @@
                     latq.at[0], lat.at[x, source], lat_send.at[0], lat_recv.at[source], {"tm": source}
                 ).wait_recv()
         group_copy(x).start()
+        forward(0, 0, 1)
         target = lax.broadcasted_iota(jnp.int32, (256, 256), 0)
         origin = lax.broadcasted_iota(jnp.int32, (256, 256), 1)
         h_, b_, g_, ch_ = target // 128, (target // 64) % 2, (target // 16) % 4, target % 16

time: 36.7 us -> 36.7 us (level)
  no operation moved by 1% of the time
where the time goes in v7:
time: 36.7 us; the launch traced here: 36.5 us
  Pallas kernels  34.8 us (95%)
  local copies, waits for them, and re-layouts  1.71 us (5%)
    pallas_call x1, Pallas kernels, sliced_shards(): pl.pallas_call(section_kernel, out_shape=jax.ShapeDtypeStruct((4 * CELLS,...  34.8 us
    unnamed x1, local copies, waits for them, and re-layouts  1.71 us

profile of v7, /device:TPU:18, one launch (start us, length us, event | category | flops | bytes accessed | tf_op | source)
XLA Modules:
  0.0 36.5 jit_solution(11902731860596074107)
XLA Ops:
  0.0 34.8 %shard_map.73 = bf16[384,384]{1,0:T(8,128)(2,1)} custom-call(bf16[16,384]{1,0:T(8,128)(2,1)} %lat_far.1, s32[8]{0:T(128)} %counts_far.1, bf16[432,384]{1,0:T(8,128)(2,1)} %bitcast.3, f32[384]{0:T(512)} %entry_bias_far.1, f32[384]{0:T(512)} %gain_far.1, f32[384]{0:T(512)} %residual_bias_far.1, bf16[27,24,384]{2,1,0:T(8,128)(2,1)} %taps_far.1), custom_call_target="tpu_custom_call" | custom-call | flops 5000000000 | bytes 2000000 | tf_op jit(solution)/shard_map/pallas_call | solution.py:523
  34.8 1.7 %copy.9 = bf16[4,6,16,384]{3,2,1,0:T(8,128)(2,1)} copy(bf16[4,6,16,384]{3,2,1,0:T(8,128)(2,1)} %bitcast.2) | data formatting | bytes 589824

commit v8 on v7

--- a/solution.py
+++ b/solution.py
@@ -238,10 +238,10 @@
                 low, high = PAIRS[p]
                 for k in range(3):
                     pieces[ch][s, 3 * n + k] = halves(3 * low + k, 3 * high + k, s)
-        for n in range(SLICES):
-            @pl.when(n != z)
-            def _():
-                z_copy(ch, n).start()
+
+            @pl.when(s != z)
+            def _():
+                z_copy(ch, s).start()
 
         @pl.when(z < SLICES)
         def _():

time: 36.7 us -> 36.7 us (level)
  no operation moved by 1% of the time
where the time goes in v8:
time: 36.7 us; the launch traced here: 36.5 us
  Pallas kernels  34.8 us (95%)
  local copies, waits for them, and re-layouts  1.71 us (5%)
    pallas_call x1, Pallas kernels, sliced_shards(): pl.pallas_call(section_kernel, out_shape=jax.ShapeDtypeStruct((4 * CELLS,...  34.8 us
    unnamed x1, local copies, waits for them, and re-layouts  1.71 us

profile of v8, /device:TPU:18, one launch (start us, length us, event | category | flops | bytes accessed | tf_op | source)
XLA Modules:
  0.0 36.5 jit_solution(16962795519815094062)
XLA Ops:
  0.0 34.8 %shard_map.73 = bf16[384,384]{1,0:T(8,128)(2,1)} custom-call(bf16[16,384]{1,0:T(8,128)(2,1)} %lat_far.1, s32[8]{0:T(128)} %counts_far.1, bf16[432,384]{1,0:T(8,128)(2,1)} %bitcast.3, f32[384]{0:T(512)} %entry_bias_far.1, f32[384]{0:T(512)} %gain_far.1, f32[384]{0:T(512)} %residual_bias_far.1, bf16[27,24,384]{2,1,0:T(8,128)(2,1)} %taps_far.1), custom_call_target="tpu_custom_call" | custom-call | flops 5000000000 | bytes 2000000 | tf_op jit(solution)/shard_map/pallas_call | solution.py:523
  34.8 1.7 %copy.9 = bf16[4,6,16,384]{3,2,1,0:T(8,128)(2,1)} copy(bf16[4,6,16,384]{3,2,1,0:T(8,128)(2,1)} %bitcast.2) | data formatting | bytes 589824
